TPU v7x, 32 devices: a whole 2x2x4 slice. The times are simulated.
32 devices in a mesh: req: 2 (over y), ctx: 16 (over z, x, core).
Axes of the slice: x: 2, y: 2, z: 4, core: 2. Of those that a mesh axis runs over, the one named last changes fastest.
Arguments:
- query_source: bfloat16 [2304, 256], P(('req', 'ctx')), parts along dimension 0, may hold values from -32 to 32
- key_source: bfloat16 [2304, 256], P(('req', 'ctx')), parts along dimension 0, may hold values from -4 to 4
- query_edit: bfloat16 [2304, 256], P(('req', 'ctx')), parts along dimension 0, may hold values from -32 to 32
- key_edit: bfloat16 [2304, 256], P(('req', 'ctx')), parts along dimension 0, may hold values from -4 to 4
- text_count: int32 [2], P('req'), parts along dimension 0, may hold values from 72 to 288, as said below
Outputs:
- query_grad: float32 [2304, 256], P(('req', 'ctx')), parts along dimension 0
- key_grad: float32 [2304, 256], P(('req', 'ctx')), parts along dimension 0
There are 2 independent parts, one for each index of `req`. A program takes and returns all parts, laid end to end along the dimension named above; each array names one. Nothing has to cross between parts.
Inputs may be any that keep to these rules, and one draw needn't show every extreme that they name: The first 288 positions are text slots; those at or past text_count are padding.
All inputs are finite; a program needn't handle non-finite values.
Results may differ from a plain program's by a relative error of at most 0.0095.
Values may be sent and summed in bfloat16 or wider, within the bound.
No kernel may reach another device: no remote copies, remote signals or barrier semaphores. Data moves between devices by JAX's collectives and lax.ppermute only.
A program may use at most 64 MiB of HBM per device.

v0:
```python
import math

import jax
import jax.numpy as jnp
from jax import lax
from jax.sharding import PartitionSpec as P

HEAD_DIM = 128


def masked_softmax(scores, key_valid):
    masked = jnp.where(key_valid, scores, -jnp.inf)
    highest = jnp.max(masked, axis=-1, keepdims=True)
    powers = jnp.where(key_valid, jnp.exp(scores - highest), 0.0)
    totals = jnp.sum(powers, axis=-1, keepdims=True)
    return (powers / totals, highest + jnp.log(totals))


def local(query_source, key_source, query_edit, key_edit, text_count):
    local_rows, full_width = query_source.shape
    head_count = full_width // HEAD_DIM
    all_rows = local_rows * lax.axis_size("ctx")
    text_slots = min(512, all_rows // 4)
    score_scale = 1.0 / math.sqrt(HEAD_DIM)
    weight = 4.0 * all_rows * math.sqrt(all_rows)
    places = jnp.arange(all_rows)
    token_valid = (places >= text_slots) | (places < text_count[0])
    own_places = lax.axis_index("ctx") * local_rows + jnp.arange(local_rows)
    own_valid = (own_places >= text_slots) | (own_places < text_count[0])
    own_weight = own_valid.astype(jnp.float32)

    def heads_view(matrix):
        return matrix.reshape(matrix.shape[0], head_count, HEAD_DIM)

    every_ks, every_ke = (
        lax.all_gather(key_source, "ctx", axis=0, tiled=True),
        lax.all_gather(key_edit, "ctx", axis=0, tiled=True),
    )
    own_qs = heads_view(query_source)
    own_qe = heads_view(query_edit)
    scores_source = (
        jnp.einsum("rhd,lhd->hrl", own_qs, heads_view(every_ks), preferred_element_type=jnp.float32)
        * score_scale
    )
    scores_edit = (
        jnp.einsum("rhd,lhd->hrl", own_qe, heads_view(every_ke), preferred_element_type=jnp.float32)
        * score_scale
    )
    probs_source, logsum_source = masked_softmax(scores_source, token_valid[None, None, :])
    probs_edit, logsum_edit = masked_softmax(scores_edit, token_valid[None, None, :])
    map_grad = 2.0 * weight * (probs_edit - probs_source) * own_weight[None, :, None]
    row_delta = jnp.sum(map_grad * probs_edit, axis=-1, keepdims=True)
    score_grad = (probs_edit * (map_grad - row_delta)).astype(jnp.bfloat16)
    query_grad = (
        jnp.einsum(
            "hrl,lhd->rhd", score_grad, heads_view(every_ke), preferred_element_type=jnp.float32
        )
        * score_scale
    )
    term_block = (
        jnp.einsum("hrl,rhd->lhd", score_grad, own_qe, preferred_element_type=jnp.float32)
        * score_scale
    )
    key_grad = lax.psum_scatter(
        term_block.reshape(local_rows * lax.axis_size("ctx"), full_width),
        "ctx",
        scatter_dimension=0,
        tiled=True,
    )
    return (query_grad.reshape(local_rows, full_width), key_grad)


def solution(mesh):
    in_specs = (
        P(("req", "ctx"), None),
        P(("req", "ctx"), None),
        P(("req", "ctx"), None),
        P(("req", "ctx"), None),
        P("req"),
    )
    out_specs = (P(("req", "ctx"), None), P(("req", "ctx"), None))
    return jax.shard_map(local, mesh=mesh, in_specs=in_specs, out_specs=out_specs, check_vma=False)
```

profile of v0, /device:TPU:0, one launch (start us, length us, event | category | flops | bytes accessed | tf_op | source)
XLA Modules:
  0.0 119.4 jit_solution(7638093069102241119)
XLA Ops:
  7.2 0.0 copy-start
  7.2 0.0 copy-start.1
  7.2 0.0 reduce-scatter.2.cloned.1.call-start
  7.9 25.1 %all_gather.7 = bf16[1152,256]{1,0:T(8,128)(2,1)S(1)} all-gather(bf16[72,256]{1,0:T(8,128)(2,1)} %param.6), channel_id=1, replica_groups=mesh['req'=2,'ctx'=16] {'ctx'}, dimensions={0}, use_global_device_ids=true | all-gather | bytes 626688 | tf_op jit(solution)/shard_map/all_gather | solution.py:36
  33.0 0.3 copy.24
  33.3 0.0 copy-done.1
  33.3 0.0 copy-start.2
  33.3 19.1 %all_gather.6 = bf16[1152,256]{1,0:T(8,128)(2,1)S(1)} all-gather(bf16[72,256]{1,0:T(8,128)(2,1)S(1)} %copy-done.1), channel_id=1, replica_groups=mesh['req'=2,'ctx'=16] {'ctx'}, dimensions={0}, use_global_device_ids=true | all-gather | bytes 626688 | tf_op jit(solution)/shard_map/all_gather | solution.py:37
  52.3 0.3 copy.21
  52.6 0.0 copy-done.2
  52.7 0.2 convolution_multiply_fusion.1
  52.9 0.0 copy-done
  52.9 0.3 convolution_multiply_fusion.2
  53.2 0.3 fusion.33
  53.5 0.5 multiply_reduce_fusion
  54.0 0.2 multiply_convert_fusion
  54.1 0.4 convolution_multiply_fusion
  54.5 1.4 %copy.30 = f32[1152,256]{1,0:T(8,128)} copy(f32[1152,256]{0,1:T(8,128)S(1)} %bitcast.40) | data formatting | bytes 2359296 | tf_op jit(solution)/shard_map/reshape | solution.py:65
  55.9 0.0 reduce-scatter.2.cloned.1.call-update
  55.9 0.4 fusion.12
  56.3 0.6 copy.50
  56.9 55.7 %reduce-scatter.2.cloned.1.call-done = f32[72,256]{1,0:T(8,128)} async-done(((f32[1152,256]{1,0:T(8,128)}), f32[72,256]{1,0:T(8,128)}) %reduce-scatter.2.cloned.1.call-update) | async-done | bytes 73744 | tf_op jit(solution)/shard_map/reduce_scatter | solution.py:64
  (2 shorter events, 0.0 us)
Async XLA Ops:
  7.2 45.7 %copy-start = (bf16[72,256]{1,0:T(8,128)(2,1)S(1)}, bf16[72,256]{1,0:T(8,128)(2,1)}, u32[]{:S(2)}) copy-start(bf16[72,256]{1,0:T(8,128)(2,1)} %param.7) | copy-start | bytes 110596
  7.2 26.1 %copy-start.1 = (bf16[72,256]{1,0:T(8,128)(2,1)S(1)}, bf16[72,256]{1,0:T(8,128)(2,1)}, u32[]{:S(2)}) copy-start(bf16[72,256]{1,0:T(8,128)(2,1)} %param.8) | copy-start | bytes 110596
  7.2 105.4 %reduce-scatter.2.cloned.1.call-start = ((), (), s32[]{:S(2)}) async-start(), calls=%async_computation.1 | async-start | bytes 1253376 | tf_op jit(solution)/shard_map/reduce_scatter | solution.py:64
  33.3 19.4 %copy-start.2 = (bf16[72,256]{1,0:T(8,128)(2,1)S(1)}, bf16[72,256]{1,0:T(8,128)(2,1)}, u32[]{:S(2)}) copy-start(bf16[72,256]{1,0:T(8,128)(2,1)} %param.5) | copy-start | bytes 110596
Sparse Core Ops, SparseCore 0:
  56.0 56.5 reduce-scatter.1
where the time goes:
time: 120 us; the launch traced here: 119 us
  waiting for transfers between devices  55.7 us (46%)
  blocking collectives  44.1 us (37%)
  between operations  14.8 us (12%)
  local copies, waits for them, and re-layouts  2.63 us (2%)
  matrix products  1.21 us (1%)
    reduce_scatter x1, waiting for transfers between devices, local(): lax.psum_scatter(term_block.reshape(local_rows * lax.axis_size('ctx'), fu...  55.7 us
    all_gather x1, blocking collectives, local(): lax.all_gather(key_source, 'ctx', axis=0, tiled=True)  25.1 us
    all_gather x1, blocking collectives, local(): lax.all_gather(key_edit, 'ctx', axis=0, tiled=True)  19.1 us
  transfers between devices with their start and end apart: 1, of which 1 were waited for; matrix products, arithmetic and copies ran while one was open for 1% of the time, Pallas kernels for 0%

commit v1 on v0

v1 whole, which is shorter than its diff:
```python
import functools
import math

import jax
import jax.numpy as jnp
from jax import lax
from jax.experimental import pallas as pl
from jax.experimental.pallas import tpu as pltpu
from jax.sharding import PartitionSpec as P

HEAD_DIM = 128
TEXT_SLOTS = 512
GATHER_ALL_ROWS = 2048
MASKED = -1e30
VMEM = pl.BlockSpec(memory_space=pltpu.VMEM)
SMEM = pl.BlockSpec(memory_space=pltpu.SMEM)


def masked_softmax(scores, key_valid):
    masked = jnp.where(key_valid, scores, -jnp.inf)
    highest = jnp.max(masked, axis=-1, keepdims=True)
    powers = jnp.where(key_valid, jnp.exp(scores - highest), 0.0)
    totals = jnp.sum(powers, axis=-1, keepdims=True)
    return powers / totals


def local_by_rows(query_source, key_source, query_edit, key_edit, text_count):
    local_rows, full_width = query_source.shape
    head_count = full_width // HEAD_DIM
    all_rows = local_rows * lax.axis_size("ctx")
    text_slots = min(TEXT_SLOTS, all_rows // 4)
    score_scale = 1.0 / math.sqrt(HEAD_DIM)
    weight = 4.0 * all_rows * math.sqrt(all_rows)
    places = jnp.arange(all_rows)
    token_valid = (places >= text_slots) | (places < text_count[0])
    own_places = lax.axis_index("ctx") * local_rows + jnp.arange(local_rows)
    own_valid = (own_places >= text_slots) | (own_places < text_count[0])
    own_weight = own_valid.astype(jnp.float32)

    def heads_view(matrix):
        return matrix.reshape(matrix.shape[0], head_count, HEAD_DIM)

    every_ks = lax.all_gather(key_source, "ctx", axis=0, tiled=True)
    every_ke = lax.all_gather(key_edit, "ctx", axis=0, tiled=True)
    own_qs, own_qe = heads_view(query_source), heads_view(query_edit)
    dot = functools.partial(jnp.einsum, preferred_element_type=jnp.float32)
    scores_source = dot("rhd,lhd->hrl", own_qs, heads_view(every_ks)) * score_scale
    scores_edit = dot("rhd,lhd->hrl", own_qe, heads_view(every_ke)) * score_scale
    probs_source = masked_softmax(scores_source, token_valid[None, None, :])
    probs_edit = masked_softmax(scores_edit, token_valid[None, None, :])
    map_grad = 2.0 * weight * (probs_edit - probs_source) * own_weight[None, :, None]
    row_delta = jnp.sum(map_grad * probs_edit, axis=-1, keepdims=True)
    score_grad = (probs_edit * (map_grad - row_delta)).astype(jnp.bfloat16)
    query_grad = dot("hrl,lhd->rhd", score_grad, heads_view(every_ke)) * score_scale
    term_block = dot("hrl,rhd->lhd", score_grad, own_qe) * score_scale
    key_grad = lax.psum_scatter(
        term_block.reshape(all_rows, full_width), "ctx", scatter_dimension=0, tiled=True
    )
    return (query_grad.reshape(local_rows, full_width), key_grad)


def pack_kernel(head_ref, qs_ref, ks_ref, qe_ref, ke_ref, own_ref, other_ref):
    first = head_ref[0] == 0
    for place, ref in enumerate((qs_ref, ks_ref, qe_ref, ke_ref)):
        low, high = ref[:, :HEAD_DIM], ref[:, HEAD_DIM:]
        columns = slice(place * HEAD_DIM, (place + 1) * HEAD_DIM)
        own_ref[:, columns] = jnp.where(first, low, high)
        other_ref[:, columns] = jnp.where(first, high, low)


def dot_nt(a, b):
    return lax.dot_general(a, b, (((1,), (1,)), ((), ())), preferred_element_type=jnp.float32)


def fold(block, op):
    parts = [block[i : i + 8] for i in range(0, block.shape[0], 8)]
    while len(parts) > 1:
        parts = [op(*parts[i : i + 2]) if i + 1 < len(parts) else parts[i] for i in range(0, len(parts), 2)]
    return parts[0]


def head_kernel(
    weight, own_rows, a_ref, b_ref, bias_ref, live_ref, live_own_ref, query_out, key_out, scores_ref, powers_ref
):
    half = a_ref.shape[0]
    rows = 2 * half
    mine = 2 * own_rows
    scale = 1.0 / math.sqrt(HEAD_DIM)
    sharp = scale * math.log2(math.e)
    blocks = rows // mine

    def part(which, start, size):
        columns = slice(which * HEAD_DIM, (which + 1) * HEAD_DIM)
        if start + size <= half:
            return a_ref[start : start + size, columns]
        if start >= half:
            return b_ref[start - half : start - half + size, columns]
        return jnp.concatenate([a_ref[start:half, columns], b_ref[: start + size - half, columns]], axis=0)

    def queries(which, start, size):
        one = (lax.broadcasted_iota(jnp.int32, (size, HEAD_DIM), 1) == 0).astype(jnp.bfloat16)
        return jnp.concatenate([part(which, start, size), one], axis=1)

    def keys(which, start, size):
        return jnp.concatenate([part(which, start, size), bias_ref[start : start + size]], axis=1)

    def own_powers(which):
        scores = dot_nt(queries(which, 0, mine), keys(which + 1, 0, rows))
        highest = jnp.max(scores, axis=1, keepdims=True)
        powers = jnp.exp2((scores - highest) * sharp)
        return powers * (1.0 / jnp.sum(powers, axis=1, keepdims=True))

    probs_source, probs_edit = own_powers(0), own_powers(2)
    map_grad = (probs_edit - probs_source) * (2.0 * weight * live_own_ref[...])
    row_delta = jnp.sum(map_grad * probs_edit, axis=1, keepdims=True)
    grad = (probs_edit * (map_grad - row_delta)).astype(jnp.bfloat16)
    query_out[...] = jnp.dot(grad, part(3, 0, rows), preferred_element_type=jnp.float32) * scale

    chunks = []
    start = 0
    while start < rows:
        size = min(256, rows - start)
        chunks.append((start, size))
        start += size

    def score(n):
        start, size = chunks[n]
        tops = []
        for m, which in enumerate((0, 2)):
            wide = queries(which, start, size)
            top = None
            for k in range(blocks):
                block = dot_nt(keys(which + 1, k * mine, mine), wide)
                scores_ref[n % 2, m, k * mine : (k + 1) * mine, :size] = block
                high = fold(block, jnp.maximum)
                top = high if top is None else jnp.maximum(top, high)
            tops.append(jnp.max(top, axis=0, keepdims=True))
        return tops

    total = jnp.zeros((mine, HEAD_DIM), jnp.float32)
    tops = score(0)
    for n, (start, size) in enumerate(chunks):
        later = score(n + 1) if n + 1 < len(chunks) else None
        sums = [None] * 4
        for k in range(blocks):
            place = slice(k * mine, (k + 1) * mine)
            source = jnp.exp2((scores_ref[n % 2, 0, place, :size] - tops[0]) * sharp)
            edit = jnp.exp2((scores_ref[n % 2, 1, place, :size] - tops[1]) * sharp)
            if k == 0:
                powers_ref[0, :, :size] = source
                powers_ref[1, :, :size] = edit
            terms = [fold(t, jnp.add) for t in (source, edit, edit * edit, source * edit)]
            sums = [t if s is None else s + t for s, t in zip(sums, terms)]
        sum_source, sum_edit, square, cross = [jnp.sum(s, axis=0, keepdims=True) for s in sums]
        over_source, over_edit = 1.0 / sum_source, 1.0 / sum_edit
        factor = 2.0 * weight * live_ref[:, start : start + size]
        delta = factor * (square * over_edit - cross * over_source) * over_edit
        probs_edit = powers_ref[1, :, :size] * over_edit
        probs_source = powers_ref[0, :, :size] * over_source
        grad = (probs_edit * (factor * (probs_edit - probs_source) - delta)).astype(jnp.bfloat16)
        total = total + jnp.dot(grad, part(2, start, size), preferred_element_type=jnp.float32)
        tops = later
    key_out[...] = total * scale


def unpack_kernel(head_ref, query_ref, key_ref, back_ref, query_out, key_out):
    first = head_ref[0] == 0
    for place, (ref, out) in enumerate(((query_ref, query_out), (key_ref, key_out))):
        own = ref[...]
        back = back_ref[:, place * HEAD_DIM : (place + 1) * HEAD_DIM]
        out[:, :HEAD_DIM] = jnp.where(first, own, back)
        out[:, HEAD_DIM:] = jnp.where(first, back, own)


def local_by_heads(query_source, key_source, query_edit, key_edit, text_count):
    local_rows, full_width = query_source.shape
    size = lax.axis_size("ctx")
    all_rows = local_rows * size
    text_slots = min(TEXT_SLOTS, all_rows // 4)
    weight = 4.0 * all_rows * math.sqrt(all_rows)
    me = lax.axis_index("ctx")
    head = (me // 2) % 2
    head_arg = head.reshape(1).astype(jnp.int32)

    def swap(array, bits):
        return lax.ppermute(array, "ctx", [(i, i ^ bits) for i in range(size)])

    pack = jax.ShapeDtypeStruct((local_rows, 4 * HEAD_DIM), jnp.bfloat16)
    own, other = pl.pallas_call(
        pack_kernel, out_shape=(pack, pack), in_specs=[SMEM] + [VMEM] * 4, out_specs=(VMEM, VMEM), name="pack"
    )(head_arg, query_source, key_source, query_edit, key_edit)
    two = jnp.concatenate([own, swap(other, 2)], axis=0)
    held = jnp.concatenate([two] + [swap(two, bits) for bits in range(4, size, 4)], axis=0)
    across = swap(held, 1)

    order = jnp.arange(all_rows)
    half = all_rows // 2
    within = order % half
    device = me ^ (order // half) ^ (within // (2 * local_rows)) * 4 ^ (within // local_rows % 2) * 2
    place = device * local_rows + order % local_rows
    live = (place >= text_slots) | (place < text_count[0])
    bias = jnp.broadcast_to(jnp.where(live, 0.0, MASKED).astype(jnp.bfloat16)[:, None], (all_rows, HEAD_DIM))
    live_row = live.astype(jnp.float32)

    mine = 2 * local_rows
    grad = jax.ShapeDtypeStruct((mine, HEAD_DIM), jnp.float32)
    query_part, key_part = pl.pallas_call(
        functools.partial(head_kernel, weight, local_rows),
        out_shape=(grad, grad),
        in_specs=[VMEM] * 5,
        out_specs=(VMEM, VMEM),
        scratch_shapes=[
            pltpu.VMEM((2, 2, all_rows, 256), jnp.float32),
            pltpu.VMEM((2, mine, 256), jnp.float32),
        ],
        compiler_params=pltpu.CompilerParams(vmem_limit_bytes=40 * 1024 * 1024),
        name="head",
    )(held, across, bias, live_row[None, :], live_row[:mine, None])
    back = swap(jnp.concatenate([query_part[local_rows:], key_part[local_rows:]], axis=1), 2)
    out = jax.ShapeDtypeStruct((local_rows, full_width), jnp.float32)
    return pl.pallas_call(
        unpack_kernel, out_shape=(out, out), in_specs=[SMEM] + [VMEM] * 3, out_specs=(VMEM, VMEM), name="unpack"
    )(head_arg, query_part[:local_rows], key_part[:local_rows], back)


def local(query_source, key_source, query_edit, key_edit, text_count):
    local_rows, full_width = query_source.shape
    size = lax.axis_size("ctx")
    small = local_rows * size <= GATHER_ALL_ROWS
    if full_width == 2 * HEAD_DIM and small and size >= 8 and size & (size - 1) == 0 and local_rows % 8 == 0:
        return local_by_heads(query_source, key_source, query_edit, key_edit, text_count)
    return local_by_rows(query_source, key_source, query_edit, key_edit, text_count)


def solution(mesh):
    split = P(("req", "ctx"), None)
    return jax.shard_map(
        local, mesh=mesh, in_specs=(split,) * 4 + (P("req"),), out_specs=(split, split), check_vma=False
    )
```

time: 120 us -> 38.5 us (0.32)
  blocking collectives: 44.1 us -> 0 us
  waiting for transfers between devices: 55.7 us -> 15.9 us
  between operations: 14.8 us -> 1.41 us
  starting transfers between devices: 0.04 us -> 9.33 us
  Pallas kernels: 0 us -> 8.82 us
  matrix products: 1.21 us -> 0 us
    reduce_scatter x1 -> x0, waiting for transfers between devices: 55.7 us -> none  [local(): lax.psum_scatter(term_block.reshape(local_rows * lax.axis_size('ctx'), fu...]
    all_gather x2 -> x0, blocking collectives: 44.1 us -> none  [the longest x1 25.1 us: local(): lax.all_gather(key_source, 'ctx', axis=0, tiled=True)]
    ppermute x0 -> x6, waiting for transfers between devices: none -> 15.9 us  [swap(): return lax.ppermute(array, 'ctx', [(i, i ^ bits) for i in range(size)])]
    ppermute x0 -> x6, starting transfers between devices: none -> 9.33 us  [swap(): return lax.ppermute(array, 'ctx', [(i, i ^ bits) for i in range(size)])]
    pallas_call x0 -> x3, Pallas kernels: none -> 8.82 us  [the longest x1 5.71 us: local_by_heads(): pl.pallas_call(functools.partial(head_kernel, weight, local_rows), out_sh...]
    reshape x2 -> x0, local copies, waits for them, and re-layouts: 2.02 us -> none  [the longest x1 1.38 us: local(): term_block.reshape(local_rows * lax.axis_size('ctx'), full_width)]
    unnamed x6 -> x5, local copies, waits for them, and re-layouts: 0.02 us -> 1.54 us
    dot_general x4 -> x0, matrix products: 1.21 us -> none  [the longest x1 0.36 us: local(): jnp.einsum('hrl,rhd->lhd', score_grad, own_qe, preferred_element_type=jnp...]
  transfers between devices with their start and end apart: 1 -> 6, of which waited for: 1 -> 5; matrix products, arithmetic and copies ran while one was open for 1% -> 3% of each run, Pallas kernels for 0% -> 0%
where the time goes in v1:
time: 38.5 us; the launch traced here: 38.2 us
  waiting for transfers between devices  15.9 us (41%)
  starting transfers between devices  9.33 us (24%)
  Pallas kernels  8.82 us (23%)
  local copies, waits for them, and re-layouts  2.53 us (7%)
  between operations  1.41 us (4%)
    ppermute x6, waiting for transfers between devices, swap(): return lax.ppermute(array, 'ctx', [(i, i ^ bits) for i in range(size)])  15.9 us
    ppermute x6, starting transfers between devices, swap(): return lax.ppermute(array, 'ctx', [(i, i ^ bits) for i in range(size)])  9.33 us
    pallas_call x1, Pallas kernels, local_by_heads(): pl.pallas_call(functools.partial(head_kernel, weight, local_rows), out_sh...  5.71 us
    pallas_call x1, Pallas kernels, local_by_heads(): pl.pallas_call(unpack_kernel, out_shape=(out, out), in_specs=[SMEM] + [VM...  1.59 us
    unnamed x5, local copies, waits for them, and re-layouts  1.54 us
    pallas_call x1, Pallas kernels, local_by_heads(): pl.pallas_call(pack_kernel, out_shape=(pack, pack), in_specs=[SMEM] + [VM...  1.51 us
  transfers between devices with their start and end apart: 6, of which 5 were waited for; matrix products, arithmetic and copies ran while one was open for 3% of the time, Pallas kernels for 0%

profile of v1, /device:TPU:0, one launch (start us, length us, event | category | flops | bytes accessed | tf_op | source)
XLA Modules:
  0.0 38.2 jit_solution(7266354275656066562)
XLA Ops:
  0.7 1.5 %pack.1 = (bf16[72,512]{1,0:T(8,128)(2,1)}, bf16[72,512]{1,0:T(8,128)(2,1)}) custom-call(s32[1]{0:T(128)} %bitcast.head_ref, bf16[72,256]{1,0:T(8,128)(2,1)} %qs_ref.1, bf16[72,256]{1,0:T(8,128)(2,1)} %ks_ref.1, bf16[72,256]{1,0:T(8,128)(2,1)} %qe_ref.1, bf16[72,256]{1,0:T(8,128)(2,1)} %ke_ref.1), custom_call_target="tpu_custom_call" | custom-call | tf_op jit(solution)/shard_map/pack/pallas_call | solution.py:189
  2.2 2.9 %collective-permute-start = (bf16[72,512]{1,0:T(8,128)(2,1)}, bf16[72,512]{1,0:T(8,128)(2,1)S(1)}, u32[]{:S(2)}, u32[]{:S(2)}) collective-permute-start(bf16[72,512]{1,0:T(8,128)(2,1)} %get-tuple-element.7), channel_id=1, source_target_pairs={{0,2},{1,3},{2,0},{3,1},{4,6},{5,7},{6,4},{7,5},{8,10},{9,11},{10,... | collective-permute-start | bytes 221192 | tf_op jit(solution)/shard_map/ppermute | solution.py:186
  5.1 0.9 %constant_dynamic-update-slice_fusion.1 = (bf16[144,512]{1,0:T(8,128)(2,1)S(1)}, bf16[576,512]{1,0:T(8,128)(2,1)S(1)}) fusion(bf16[72,512]{1,0:T(8,128)(2,1)} %get-tuple-element.6), kind=kLoop, calls=%fused_computation.11 | loop fusion | bytes 221184
  6.0 1.6 %collective-permute-done = bf16[72,512]{1,0:T(8,128)(2,1)S(1)} collective-permute-done((bf16[72,512]{1,0:T(8,128)(2,1)}, bf16[72,512]{1,0:T(8,128)(2,1)S(1)}, u32[]{:S(2)}, u32[]{:S(2)}) %collective-permute-start) | collective-permute-done | bytes 73760 | tf_op jit(solution)/shard_map/ppermute | solution.py:186
  7.7 2.2 %collective-permute-start.1 = (bf16[144,512]{1,0:T(8,128)(2,1)S(1)}, bf16[144,512]{1,0:T(8,128)(2,1)S(1)}, u32[]{:S(2)}, u32[]{:S(2)}) collective-permute-start(bf16[144,512]{1,0:T(8,128)(2,1)S(1)} %get-tuple-element.14), channel_id=1, source_target_pairs={{0,4},{1,5},{2,6},{3,7},{4,0},{5,1},{6,2},{7,3},{8,12},{9,13},{10,... | collective-permute-start | bytes 442376 | tf_op jit(solution)/shard_map/ppermute | solution.py:186
  9.8 2.6 %collective-permute-start.2 = (bf16[144,512]{1,0:T(8,128)(2,1)S(1)}, bf16[144,512]{1,0:T(8,128)(2,1)S(1)}, u32[]{:S(2)}, u32[]{:S(2)}) collective-permute-start(bf16[144,512]{1,0:T(8,128)(2,1)S(1)} %get-tuple-element.14), channel_id=1, source_target_pairs={{0,8},{1,9},{2,10},{3,11},{4,12},{5,13},{6,14},{7,15},{8,0},{9,1},... | collective-permute-start | bytes 442376 | tf_op jit(solution)/shard_map/ppermute | solution.py:186
  13.1 0.1 collective-permute-start.3
  13.2 1.4 %collective-permute-done.1 = bf16[144,512]{1,0:T(8,128)(2,1)S(1)} collective-permute-done((bf16[144,512]{1,0:T(8,128)(2,1)S(1)}, bf16[144,512]{1,0:T(8,128)(2,1)S(1)}, u32[]{:S(2)}, u32[]{:S(2)}) %collective-permute-start.1) | collective-permute-done | bytes 147488 | tf_op jit(solution)/shard_map/ppermute | solution.py:186
  14.6 8.2 %collective-permute-done.2 = bf16[144,512]{1,0:T(8,128)(2,1)S(1)} collective-permute-done((bf16[144,512]{1,0:T(8,128)(2,1)S(1)}, bf16[144,512]{1,0:T(8,128)(2,1)S(1)}, u32[]{:S(2)}, u32[]{:S(2)}) %collective-permute-start.2) | collective-permute-done | bytes 147488 | tf_op jit(solution)/shard_map/ppermute | solution.py:186
  22.9 0.0 collective-permute-done.3
  22.9 0.1 collective-permute-start.4
  23.0 0.1 copy.7.live_own_ref
  23.2 0.1 or_convert_fusion.live_ref
  23.3 1.7 %collective-permute-done.4.b_ref = bf16[576,512]{1,0:T(8,128)(2,1)S(1)} collective-permute-done((bf16[576,512]{1,0:T(8,128)(2,1)S(1)}, bf16[576,512]{1,0:T(8,128)(2,1)S(1)}, u32[]{:S(2)}, u32[]{:S(2)}) %collective-permute-start.4) | collective-permute-done | bytes 589856 | tf_op jit(solution)/shard_map/ppermute | solution.py:186
  25.0 0.2 broadcast_in_dim.22.bias_ref
  25.2 5.7 %head.1 = (f32[144,128]{1,0:T(8,128)S(1)}, f32[144,128]{1,0:T(8,128)S(1)}) custom-call(bf16[576,512]{1,0:T(8,128)(2,1)S(1)} %constant_dynamic-update-slice_fusion.2.a_ref, bf16[576,512]{1,0:T(8,128)(2,1)S(1)} %collective-permute-done.4.b_ref, bf16[1152,128]{1,0:T(8,128)(2,1)S(1)} %broadcast_in_dim.22.bias_ref, f32[1,1152]{1,0:T(1,128)S(1)} %or_convert_fusion.live_ref, ...), custom_call_target="tpu_custom_call" | custom-call | tf_op jit(solution)/shard_map/head/pallas_call | solution.py:207
  30.9 0.6 %fusion.34 = (f32[72,128]{1,0:T(8,128)S(1)}, f32[72,128]{1,0:T(8,128)}, f32[72,128]{1,0:T(8,128)}, f32[72,128]{1,0:T(8,128)S(1)}) fusion(f32[144,128]{1,0:T(8,128)S(1)} %get-tuple-element.8, f32[144,128]{1,0:T(8,128)S(1)} %get-tuple-element.9), kind=kLoop, calls=%fused_computation.68 | loop fusion | bytes 294912 | tf_op jit(solution)/shard_map/slice | solution.py:219
  31.6 1.5 %collective-permute-start.5 = (f32[72,256]{1,0:T(8,128)S(1)}, f32[72,256]{1,0:T(8,128)S(1)}, u32[]{:S(2)}, u32[]{:S(2)}) collective-permute-start(f32[72,256]{1,0:T(8,128)S(1)} %pad_maximum_fusion), channel_id=1, source_target_pairs={{0,2},{1,3},{2,0},{3,1},{4,6},{5,7},{6,4},{7,5},{8,10},{9,11},{10,... | collective-permute-start | bytes 221192 | tf_op jit(solution)/shard_map/ppermute | solution.py:186
  33.0 2.9 %collective-permute-done.5.back_ref = f32[72,256]{1,0:T(8,128)S(1)} collective-permute-done((f32[72,256]{1,0:T(8,128)S(1)}, f32[72,256]{1,0:T(8,128)S(1)}, u32[]{:S(2)}, u32[]{:S(2)}) %collective-permute-start.5) | collective-permute-done | bytes 73760 | tf_op jit(solution)/shard_map/ppermute | solution.py:186
  36.0 0.0 copy-start
  36.0 0.6 %copy-done = f32[72,256]{1,0:T(8,128)} copy-done((f32[72,256]{1,0:T(8,128)}, f32[72,256]{1,0:T(8,128)S(1)}, u32[]{:S(2)}) %copy-start) | copy-done | bytes 73752
  36.6 1.6 %unpack.1 = (f32[72,256]{1,0:T(8,128)}, f32[72,256]{1,0:T(8,128)}) custom-call(s32[1]{0:T(128)} %bitcast.head_ref, f32[72,128]{1,0:T(8,128)} %get-tuple-element.11.query_ref, f32[72,128]{1,0:T(8,128)} %get-tuple-element.18.key_ref, f32[72,256]{1,0:T(8,128)} %copy-done), custom_call_target="tpu_custom_call" | custom-call | tf_op jit(solution)/shard_map/unpack/pallas_call | solution.py:221
  (8 shorter events, 0.1 us)
Async XLA Ops:
  2.2 5.5 %collective-permute-start = (bf16[72,512]{1,0:T(8,128)(2,1)}, bf16[72,512]{1,0:T(8,128)(2,1)S(1)}, u32[]{:S(2)}, u32[]{:S(2)}) collective-permute-start(bf16[72,512]{1,0:T(8,128)(2,1)} %get-tuple-element.7), channel_id=1, source_target_pairs={{0,2},{1,3},{2,0},{3,1},{4,6},{5,7},{6,4},{7,5},{8,10},{9,11},{10,... | collective-permute-start | bytes 221192 | tf_op jit(solution)/shard_map/ppermute | solution.py:186
  7.7 6.9 %collective-permute-start.1 = (bf16[144,512]{1,0:T(8,128)(2,1)S(1)}, bf16[144,512]{1,0:T(8,128)(2,1)S(1)}, u32[]{:S(2)}, u32[]{:S(2)}) collective-permute-start(bf16[144,512]{1,0:T(8,128)(2,1)S(1)} %get-tuple-element.14), channel_id=1, source_target_pairs={{0,4},{1,5},{2,6},{3,7},{4,0},{5,1},{6,2},{7,3},{8,12},{9,13},{10,... | collective-permute-start | bytes 442376 | tf_op jit(solution)/shard_map/ppermute | solution.py:186
  9.8 13.0 %collective-permute-start.2 = (bf16[144,512]{1,0:T(8,128)(2,1)S(1)}, bf16[144,512]{1,0:T(8,128)(2,1)S(1)}, u32[]{:S(2)}, u32[]{:S(2)}) collective-permute-start(bf16[144,512]{1,0:T(8,128)(2,1)S(1)} %get-tuple-element.14), channel_id=1, source_target_pairs={{0,8},{1,9},{2,10},{3,11},{4,12},{5,13},{6,14},{7,15},{8,0},{9,1},... | collective-permute-start | bytes 442376 | tf_op jit(solution)/shard_map/ppermute | solution.py:186
  13.1 9.8 %collective-permute-start.3 = (bf16[144,512]{1,0:T(8,128)(2,1)S(1)}, bf16[144,512]{1,0:T(8,128)(2,1)S(1)}, u32[]{:S(2)}, u32[]{:S(2)}) collective-permute-start(bf16[144,512]{1,0:T(8,128)(2,1)S(1)} %get-tuple-element.14), channel_id=1, source_target_pairs={{0,12},{1,13},{2,14},{3,15},{4,8},{5,9},{6,10},{7,11},{8,4},{9,5},... | collective-permute-start | bytes 442376 | tf_op jit(solution)/shard_map/ppermute | solution.py:186
  22.9 2.1 %collective-permute-start.4 = (bf16[576,512]{1,0:T(8,128)(2,1)S(1)}, bf16[576,512]{1,0:T(8,128)(2,1)S(1)}, u32[]{:S(2)}, u32[]{:S(2)}) collective-permute-start(bf16[576,512]{1,0:T(8,128)(2,1)S(1)} %constant_dynamic-update-slice_fusion.2.a_ref), channel_id=1, source_target_pairs={{0,1},{1,0},{2,3},{3,2},{4,5},{5,4},{6,7},{7,6},{8,9},{9,8},{10,11... | collective-permute-start | bytes 1769480 | tf_op jit(solution)/shard_map/ppermute | solution.py:186
  31.6 4.4 %collective-permute-start.5 = (f32[72,256]{1,0:T(8,128)S(1)}, f32[72,256]{1,0:T(8,128)S(1)}, u32[]{:S(2)}, u32[]{:S(2)}) collective-permute-start(f32[72,256]{1,0:T(8,128)S(1)} %pad_maximum_fusion), channel_id=1, source_target_pairs={{0,2},{1,3},{2,0},{3,1},{4,6},{5,7},{6,4},{7,5},{8,10},{9,11},{10,... | collective-permute-start | bytes 221192 | tf_op jit(solution)/shard_map/ppermute | solution.py:186
  36.0 0.6 %copy-start = (f32[72,256]{1,0:T(8,128)}, f32[72,256]{1,0:T(8,128)S(1)}, u32[]{:S(2)}) copy-start(f32[72,256]{1,0:T(8,128)S(1)} %collective-permute-done.5.back_ref) | copy-start | bytes 221188

commit v2 on v1

--- a/solution.py
+++ b/solution.py
@@ -14,6 +14,7 @@
 MASKED = -1e30
 VMEM = pl.BlockSpec(memory_space=pltpu.VMEM)
 SMEM = pl.BlockSpec(memory_space=pltpu.SMEM)
+HBM = pl.BlockSpec(memory_space=pltpu.HBM)
 
 
 def masked_softmax(scores, key_valid):
@@ -59,10 +60,17 @@
     return (query_grad.reshape(local_rows, full_width), key_grad)
 
 
-def pack_kernel(head_ref, qs_ref, ks_ref, qe_ref, ke_ref, own_ref, other_ref):
+def pack_kernel(head_ref, qs_ref, ks_ref, qe_ref, ke_ref, own_ref, other_ref, held_ref, sems):
+    copies = [
+        pltpu.make_async_copy(ref, held_ref.at[place], sems.at[place])
+        for place, ref in enumerate((qs_ref, ks_ref, qe_ref, ke_ref))
+    ]
+    for copy in copies:
+        copy.start()
     first = head_ref[0] == 0
-    for place, ref in enumerate((qs_ref, ks_ref, qe_ref, ke_ref)):
-        low, high = ref[:, :HEAD_DIM], ref[:, HEAD_DIM:]
+    for place, copy in enumerate(copies):
+        copy.wait()
+        low, high = held_ref[place, :, :HEAD_DIM], held_ref[place, :, HEAD_DIM:]
         columns = slice(place * HEAD_DIM, (place + 1) * HEAD_DIM)
         own_ref[:, columns] = jnp.where(first, low, high)
         other_ref[:, columns] = jnp.where(first, high, low)
@@ -80,7 +88,7 @@
 
 
 def head_kernel(
-    weight, own_rows, a_ref, b_ref, bias_ref, live_ref, live_own_ref, query_out, key_out, scores_ref, powers_ref
+    weight, own_rows, a_ref, b_ref, bias_ref, live_ref, live_own_ref, keep_out, send_out, scores_ref, powers_ref
 ):
     half = a_ref.shape[0]
     rows = 2 * half
@@ -114,7 +122,7 @@
     map_grad = (probs_edit - probs_source) * (2.0 * weight * live_own_ref[...])
     row_delta = jnp.sum(map_grad * probs_edit, axis=1, keepdims=True)
     grad = (probs_edit * (map_grad - row_delta)).astype(jnp.bfloat16)
-    query_out[...] = jnp.dot(grad, part(3, 0, rows), preferred_element_type=jnp.float32) * scale
+    query_grad = jnp.dot(grad, part(3, 0, rows), preferred_element_type=jnp.float32) * scale
 
     chunks = []
     start = 0
@@ -129,9 +137,9 @@
         for m, which in enumerate((0, 2)):
             wide = queries(which, start, size)
             top = None
-            for k in range(blocks):
-                block = dot_nt(keys(which + 1, k * mine, mine), wide)
-                scores_ref[n % 2, m, k * mine : (k + 1) * mine, :size] = block
+            for k in range(0, rows, half):
+                block = dot_nt(keys(which + 1, k, half), wide)
+                scores_ref[n % 2, m, k : k + half, :size] = block
                 high = fold(block, jnp.maximum)
                 top = high if top is None else jnp.maximum(top, high)
             tops.append(jnp.max(top, axis=0, keepdims=True))
@@ -160,16 +168,9 @@
         grad = (probs_edit * (factor * (probs_edit - probs_source) - delta)).astype(jnp.bfloat16)
         total = total + jnp.dot(grad, part(2, start, size), preferred_element_type=jnp.float32)
         tops = later
-    key_out[...] = total * scale
-
-
-def unpack_kernel(head_ref, query_ref, key_ref, back_ref, query_out, key_out):
-    first = head_ref[0] == 0
-    for place, (ref, out) in enumerate(((query_ref, query_out), (key_ref, key_out))):
-        own = ref[...]
-        back = back_ref[:, place * HEAD_DIM : (place + 1) * HEAD_DIM]
-        out[:, :HEAD_DIM] = jnp.where(first, own, back)
-        out[:, HEAD_DIM:] = jnp.where(first, back, own)
+    for columns, grad in ((slice(None, HEAD_DIM), query_grad), (slice(HEAD_DIM, None), total * scale)):
+        keep_out[:, columns] = grad[:own_rows]
+        send_out[:, columns] = grad[own_rows:]
 
 
 def local_by_heads(query_source, key_source, query_edit, key_edit, text_count):
@@ -179,34 +180,49 @@
     text_slots = min(TEXT_SLOTS, all_rows // 4)
     weight = 4.0 * all_rows * math.sqrt(all_rows)
     me = lax.axis_index("ctx")
-    head = (me // 2) % 2
-    head_arg = head.reshape(1).astype(jnp.int32)
+    head = (me >> 1) & 1
+    arrays = (query_source, key_source, query_edit, key_edit)
 
     def swap(array, bits):
         return lax.ppermute(array, "ctx", [(i, i ^ bits) for i in range(size)])
 
     pack = jax.ShapeDtypeStruct((local_rows, 4 * HEAD_DIM), jnp.bfloat16)
     own, other = pl.pallas_call(
-        pack_kernel, out_shape=(pack, pack), in_specs=[SMEM] + [VMEM] * 4, out_specs=(VMEM, VMEM), name="pack"
-    )(head_arg, query_source, key_source, query_edit, key_edit)
-    two = jnp.concatenate([own, swap(other, 2)], axis=0)
-    held = jnp.concatenate([two] + [swap(two, bits) for bits in range(4, size, 4)], axis=0)
-    across = swap(held, 1)
-
+        pack_kernel,
+        out_shape=(pack, pack),
+        in_specs=[SMEM] + [HBM] * 4,
+        out_specs=(VMEM, VMEM),
+        scratch_shapes=[pltpu.VMEM((4, local_rows, full_width), jnp.bfloat16), pltpu.SemaphoreType.DMA((4,))],
+        compiler_params=pltpu.CompilerParams(vmem_limit_bytes=4 * 1024 * 1024),
+        name="pack",
+    )(head.reshape(1), *(pltpu.with_memory_space_constraint(x, pltpu.HBM) for x in arrays))
+
+    mine = 2 * local_rows
     order = jnp.arange(all_rows)
     half = all_rows // 2
     within = order % half
-    device = me ^ (order // half) ^ (within // (2 * local_rows)) * 4 ^ (within // local_rows % 2) * 2
+    device = me ^ (order // half) ^ (within // mine) * 4 ^ (within // local_rows % 2) * 2
     place = device * local_rows + order % local_rows
     live = (place >= text_slots) | (place < text_count[0])
     bias = jnp.broadcast_to(jnp.where(live, 0.0, MASKED).astype(jnp.bfloat16)[:, None], (all_rows, HEAD_DIM))
     live_row = live.astype(jnp.float32)
-
-    mine = 2 * local_rows
-    grad = jax.ShapeDtypeStruct((mine, HEAD_DIM), jnp.float32)
-    query_part, key_part = pl.pallas_call(
+    live_own = live_row[:mine, None]
+
+    partner, bias, live_row, live_own = lax.optimization_barrier(
+        (swap(other, 2), bias, live_row[None, :], live_own)
+    )
+    two = jnp.concatenate([own, partner], axis=0)
+    far = [(0, own), (local_rows, partner)]
+    for bit in [1 << p for p in range(size.bit_length() - 2, 2, -1)]:
+        far += [(at + bit * mine // 4, swap(block, bit)) for at, block in far]
+    far = far[2:]
+    blocks = [(0, two), (mine, swap(two, 4))] + far + [(at + mine, swap(block, 4)) for at, block in far]
+    held = jnp.concatenate([block for _, block in sorted(blocks, key=lambda entry: entry[0])], axis=0)
+
+    grads = jax.ShapeDtypeStruct((local_rows, 2 * HEAD_DIM), jnp.float32)
+    keep, send = pl.pallas_call(
         functools.partial(head_kernel, weight, local_rows),
-        out_shape=(grad, grad),
+        out_shape=(grads, grads),
         in_specs=[VMEM] * 5,
         out_specs=(VMEM, VMEM),
         scratch_shapes=[
@@ -215,12 +231,16 @@
         ],
         compiler_params=pltpu.CompilerParams(vmem_limit_bytes=40 * 1024 * 1024),
         name="head",
-    )(held, across, bias, live_row[None, :], live_row[:mine, None])
-    back = swap(jnp.concatenate([query_part[local_rows:], key_part[local_rows:]], axis=1), 2)
-    out = jax.ShapeDtypeStruct((local_rows, full_width), jnp.float32)
-    return pl.pallas_call(
-        unpack_kernel, out_shape=(out, out), in_specs=[SMEM] + [VMEM] * 3, out_specs=(VMEM, VMEM), name="unpack"
-    )(head_arg, query_part[:local_rows], key_part[:local_rows], back)
+    )(held, swap(held, 1), bias, live_row, live_own)
+    back = swap(send, 2)
+
+    def both_heads(columns):
+        mine, other = keep[:, columns], back[:, columns]
+        return jnp.where(
+            head == 0, jnp.concatenate([mine, other], axis=1), jnp.concatenate([other, mine], axis=1)
+        )
+
+    return both_heads(slice(None, HEAD_DIM)), both_heads(slice(HEAD_DIM, None))
 
 
 def local(query_source, key_source, query_edit, key_edit, text_count):

time: 38.5 us -> 31.8 us (0.83)
  waiting for transfers between devices: 15.9 us -> 10.2 us
  starting transfers between devices: 9.33 us -> 12.9 us
  Pallas kernels: 8.82 us -> 5.78 us
  local copies, waits for them, and re-layouts: 2.53 us -> 0.38 us
  other arithmetic: 0.19 us -> 0.86 us
    ppermute x6 -> x8, waiting for transfers between devices: 15.9 us -> 10.2 us  [swap(): return lax.ppermute(array, 'ctx', [(i, i ^ bits) for i in range(size)])]
    ppermute x6 -> x8, starting transfers between devices: 9.33 us -> 12.9 us  [swap(): return lax.ppermute(array, 'ctx', [(i, i ^ bits) for i in range(size)])]
    pallas_call x2 -> x1, Pallas kernels: 3.1 us -> 0.86 us  [local_by_heads(): pl.pallas_call(pack_kernel, out_shape=(pack, pack), in_specs=[SMEM] + [HB...]
    unnamed x5 -> x6, local copies, waits for them, and re-layouts: 1.54 us -> 0.04 us
    pallas_call x1, Pallas kernels: 5.71 us -> 4.92 us  [local_by_heads(): pl.pallas_call(functools.partial(head_kernel, weight, local_rows), out_sh...]
    select_n x0 -> x1, other arithmetic: none -> 0.67 us  [both_heads(): jnp.where(head == 0, jnp.concatenate([mine, other], axis=1), jnp.concaten...]
    slice x1 -> x2, local copies, waits for them, and re-layouts: 0.65 us -> 0.01 us  [both_heads(): mine, other = (keep[:, columns], back[:, columns])]
  transfers between devices with their start and end apart: 6 -> 8, of which waited for: 5 -> 4; matrix products, arithmetic and copies ran while one was open for 3% -> 2% of each run, Pallas kernels for 0% -> 0%
where the time goes in v2:
time: 31.8 us; the launch traced here: 31.6 us
  starting transfers between devices  12.9 us (41%)
  waiting for transfers between devices  10.2 us (32%)
  Pallas kernels  5.78 us (18%)
  between operations  1.42 us (4%)
  other arithmetic  0.86 us (3%)
  local copies, waits for them, and re-layouts  0.38 us (1%)
    ppermute x8, starting transfers between devices, swap(): return lax.ppermute(array, 'ctx', [(i, i ^ bits) for i in range(size)])  12.9 us
    ppermute x8, waiting for transfers between devices, swap(): return lax.ppermute(array, 'ctx', [(i, i ^ bits) for i in range(size)])  10.2 us
    pallas_call x1, Pallas kernels, local_by_heads(): pl.pallas_call(functools.partial(head_kernel, weight, local_rows), out_sh...  4.92 us
    pallas_call x1, Pallas kernels, local_by_heads(): pl.pallas_call(pack_kernel, out_shape=(pack, pack), in_specs=[SMEM] + [HB...  0.86 us
    select_n x1, other arithmetic, both_heads(): jnp.where(head == 0, jnp.concatenate([mine, other], axis=1), jnp.concaten...  0.67 us
  transfers between devices with their start and end apart: 8, of which 4 were waited for; matrix products, arithmetic and copies ran while one was open for 2% of the time, Pallas kernels for 0%

profile of v2, /device:TPU:0, one launch (start us, length us, event | category | flops | bytes accessed | tf_op | source)
XLA Modules:
  0.0 31.6 jit_solution(14756369307224152550)
XLA Ops:
  0.6 0.9 %pack.1 = (bf16[72,512]{1,0:T(8,128)(2,1)S(1)}, bf16[72,512]{1,0:T(8,128)(2,1)S(1)}) custom-call(s32[1]{0:T(128)} %bitcast.head_ref, bf16[72,256]{1,0:T(8,128)(2,1)} %qs_ref.1, bf16[72,256]{1,0:T(8,128)(2,1)} %ks_ref.1, bf16[72,256]{1,0:T(8,128)(2,1)} %qe_ref.1, bf16[72,256]{1,0:T(8,128)(2,1)} %ke_ref.1), custom_call_target="tpu_custom_call" | custom-call | tf_op jit(solution)/shard_map/pack/pallas_call | solution.py:190
  1.5 3.0 %collective-permute-start = (bf16[72,512]{1,0:T(8,128)(2,1)S(1)}, bf16[72,512]{1,0:T(8,128)(2,1)S(1)}, u32[]{:S(2)}, u32[]{:S(2)}) collective-permute-start(bf16[72,512]{1,0:T(8,128)(2,1)S(1)} %get-tuple-element.11), channel_id=1, source_target_pairs={{0,2},{1,3},{2,0},{3,1},{4,6},{5,7},{6,4},{7,5},{8,10},{9,11},{10,... | collective-permute-start | bytes 221192 | tf_op jit(solution)/shard_map/ppermute | solution.py:187
  4.5 2.6 %collective-permute-start.2 = (bf16[72,512]{1,0:T(8,128)(2,1)S(1)}, bf16[72,512]{1,0:T(8,128)(2,1)S(1)}, u32[]{:S(2)}, u32[]{:S(2)}) collective-permute-start(bf16[72,512]{1,0:T(8,128)(2,1)S(1)} %get-tuple-element.10), channel_id=1, source_target_pairs={{0,8},{1,9},{2,10},{3,11},{4,12},{5,13},{6,14},{7,15},{8,0},{9,1},... | collective-permute-start | bytes 221192 | tf_op jit(solution)/shard_map/ppermute | solution.py:187
  7.8 0.1 or_convert_fusion.live_ref
  8.0 0.0 collective-permute-done
  8.0 0.2 broadcast_in_dim.23.bias_ref
  8.2 1.6 %collective-permute-start.1 = (bf16[144,512]{1,0:T(8,128)(2,1)S(1)}, bf16[144,512]{1,0:T(8,128)(2,1)S(1)}, u32[]{:S(2)}, u32[]{:S(2)}) collective-permute-start(bf16[144,512]{1,0:T(8,128)(2,1)S(1)} %pad_maximum_fusion), channel_id=1, source_target_pairs={{0,4},{1,5},{2,6},{3,7},{4,0},{5,1},{6,2},{7,3},{8,12},{9,13},{10,... | collective-permute-start | bytes 442376 | tf_op jit(solution)/shard_map/ppermute | solution.py:187
  9.9 2.0 %collective-permute-start.3 = (bf16[72,512]{1,0:T(8,128)(2,1)S(1)}, bf16[72,512]{1,0:T(8,128)(2,1)S(1)}, u32[]{:S(2)}, u32[]{:S(2)}) collective-permute-start(bf16[72,512]{1,0:T(8,128)(2,1)S(1)} %collective-permute-done), channel_id=1, source_target_pairs={{0,8},{1,9},{2,10},{3,11},{4,12},{5,13},{6,14},{7,15},{8,0},{9,1},... | collective-permute-start | bytes 221192 | tf_op jit(solution)/shard_map/ppermute | solution.py:187
  11.9 0.0 collective-permute-done.2
  11.9 0.5 %collective-permute-start.4 = (bf16[72,512]{1,0:T(8,128)(2,1)S(1)}, bf16[72,512]{1,0:T(8,128)(2,1)S(1)}, u32[]{:S(2)}, u32[]{:S(2)}) collective-permute-start(bf16[72,512]{1,0:T(8,128)(2,1)S(1)} %collective-permute-done.2), channel_id=1, source_target_pairs={{0,4},{1,5},{2,6},{3,7},{4,0},{5,1},{6,2},{7,3},{8,12},{9,13},{10,... | collective-permute-start | bytes 221192 | tf_op jit(solution)/shard_map/ppermute | solution.py:187
  12.3 2.9 %collective-permute-done.3 = bf16[72,512]{1,0:T(8,128)(2,1)S(1)} collective-permute-done((bf16[72,512]{1,0:T(8,128)(2,1)S(1)}, bf16[72,512]{1,0:T(8,128)(2,1)S(1)}, u32[]{:S(2)}, u32[]{:S(2)}) %collective-permute-start.3) | collective-permute-done | bytes 73760 | tf_op jit(solution)/shard_map/ppermute | solution.py:187
  15.2 1.9 %collective-permute-start.5 = (bf16[72,512]{1,0:T(8,128)(2,1)S(1)}, bf16[72,512]{1,0:T(8,128)(2,1)S(1)}, u32[]{:S(2)}, u32[]{:S(2)}) collective-permute-start(bf16[72,512]{1,0:T(8,128)(2,1)S(1)} %collective-permute-done.3), channel_id=1, source_target_pairs={{0,4},{1,5},{2,6},{3,7},{4,0},{5,1},{6,2},{7,3},{8,12},{9,13},{10,... | collective-permute-start | bytes 221192 | tf_op jit(solution)/shard_map/ppermute | solution.py:187
  17.1 0.0 collective-permute-done.1
  17.1 0.0 collective-permute-done.4
  17.2 2.4 %collective-permute-done.5 = bf16[72,512]{1,0:T(8,128)(2,1)S(1)} collective-permute-done((bf16[72,512]{1,0:T(8,128)(2,1)S(1)}, bf16[72,512]{1,0:T(8,128)(2,1)S(1)}, u32[]{:S(2)}, u32[]{:S(2)}) %collective-permute-start.5) | collective-permute-done | bytes 73760 | tf_op jit(solution)/shard_map/ppermute | solution.py:187
  19.6 0.0 collective-permute-start.6
  19.6 0.1 copy.7.live_own_ref
  19.7 1.9 %collective-permute-done.6.b_ref = bf16[576,512]{1,0:T(8,128)(2,1)S(1)} collective-permute-done((bf16[576,512]{1,0:T(8,128)(2,1)S(1)}, bf16[576,512]{1,0:T(8,128)(2,1)S(1)}, u32[]{:S(2)}, u32[]{:S(2)}) %collective-permute-start.6) | collective-permute-done | bytes 589856 | tf_op jit(solution)/shard_map/ppermute | solution.py:187
  21.6 4.9 %head.1 = (f32[72,256]{1,0:T(8,128)S(1)}, f32[72,256]{1,0:T(8,128)S(1)}) custom-call(bf16[576,512]{1,0:T(8,128)(2,1)S(1)} %constant_dynamic-update-slice_fusion.a_ref, bf16[576,512]{1,0:T(8,128)(2,1)S(1)} %collective-permute-done.6.b_ref, bf16[1152,128]{1,0:T(8,128)(2,1)S(1)} %broadcast_in_dim.23.bias_ref, f32[1,1152]{1,0:T(1,128)S(1)} %or_convert_fusion.live_ref, ...), custom_call_target="tpu_custom_call" | custom-call | tf_op jit(solution)/shard_map/head/pallas_call | solution.py:223
  26.5 1.4 %collective-permute-start.7 = (f32[72,256]{1,0:T(8,128)S(1)}, f32[72,256]{1,0:T(8,128)S(1)}, u32[]{:S(2)}, u32[]{:S(2)}) collective-permute-start(f32[72,256]{1,0:T(8,128)S(1)} %get-tuple-element.17), channel_id=1, source_target_pairs={{0,2},{1,3},{2,0},{3,1},{4,6},{5,7},{6,4},{7,5},{8,10},{9,11},{10,... | collective-permute-start | bytes 221192 | tf_op jit(solution)/shard_map/ppermute | solution.py:187
  27.9 3.0 %collective-permute-done.7 = f32[72,256]{1,0:T(8,128)S(1)} collective-permute-done((f32[72,256]{1,0:T(8,128)S(1)}, f32[72,256]{1,0:T(8,128)S(1)}, u32[]{:S(2)}, u32[]{:S(2)}) %collective-permute-start.7) | collective-permute-done | bytes 73760 | tf_op jit(solution)/shard_map/ppermute | solution.py:187
  30.9 0.7 %maximum_select_fusion = (f32[72,256]{1,0:T(8,128)}, f32[72,256]{1,0:T(8,128)}) fusion(f32[72,128]{1,0:T(8,128)S(1)} %get-tuple-element.21, f32[72,128]{1,0:T(8,128)S(1)} %get-tuple-element.19, pred[]{:T(512)S(6)} %eq.8, f32[72,128]{1,0:T(8,128)S(1)} %get-tuple-element.18, f32[72,128]{1,0:T(8,128)S(1)} %get-tuple-element.20), kind=kLoop, calls=%fused_computation.1 | loop fusion | flops 110592 | bytes 294913 | tf_op jit(solution)/shard_map/jit(_where)/select_n | solution.py:239
  (13 shorter events, 0.2 us)
Async XLA Ops:
  1.5 6.5 %collective-permute-start = (bf16[72,512]{1,0:T(8,128)(2,1)S(1)}, bf16[72,512]{1,0:T(8,128)(2,1)S(1)}, u32[]{:S(2)}, u32[]{:S(2)}) collective-permute-start(bf16[72,512]{1,0:T(8,128)(2,1)S(1)} %get-tuple-element.11), channel_id=1, source_target_pairs={{0,2},{1,3},{2,0},{3,1},{4,6},{5,7},{6,4},{7,5},{8,10},{9,11},{10,... | collective-permute-start | bytes 221192 | tf_op jit(solution)/shard_map/ppermute | solution.py:187
  4.5 7.3 %collective-permute-start.2 = (bf16[72,512]{1,0:T(8,128)(2,1)S(1)}, bf16[72,512]{1,0:T(8,128)(2,1)S(1)}, u32[]{:S(2)}, u32[]{:S(2)}) collective-permute-start(bf16[72,512]{1,0:T(8,128)(2,1)S(1)} %get-tuple-element.10), channel_id=1, source_target_pairs={{0,8},{1,9},{2,10},{3,11},{4,12},{5,13},{6,14},{7,15},{8,0},{9,1},... | collective-permute-start | bytes 221192 | tf_op jit(solution)/shard_map/ppermute | solution.py:187
  8.2 8.9 %collective-permute-start.1 = (bf16[144,512]{1,0:T(8,128)(2,1)S(1)}, bf16[144,512]{1,0:T(8,128)(2,1)S(1)}, u32[]{:S(2)}, u32[]{:S(2)}) collective-permute-start(bf16[144,512]{1,0:T(8,128)(2,1)S(1)} %pad_maximum_fusion), channel_id=1, source_target_pairs={{0,4},{1,5},{2,6},{3,7},{4,0},{5,1},{6,2},{7,3},{8,12},{9,13},{10,... | collective-permute-start | bytes 442376 | tf_op jit(solution)/shard_map/ppermute | solution.py:187
  9.9 5.4 %collective-permute-start.3 = (bf16[72,512]{1,0:T(8,128)(2,1)S(1)}, bf16[72,512]{1,0:T(8,128)(2,1)S(1)}, u32[]{:S(2)}, u32[]{:S(2)}) collective-permute-start(bf16[72,512]{1,0:T(8,128)(2,1)S(1)} %collective-permute-done), channel_id=1, source_target_pairs={{0,8},{1,9},{2,10},{3,11},{4,12},{5,13},{6,14},{7,15},{8,0},{9,1},... | collective-permute-start | bytes 221192 | tf_op jit(solution)/shard_map/ppermute | solution.py:187
  11.9 5.3 %collective-permute-start.4 = (bf16[72,512]{1,0:T(8,128)(2,1)S(1)}, bf16[72,512]{1,0:T(8,128)(2,1)S(1)}, u32[]{:S(2)}, u32[]{:S(2)}) collective-permute-start(bf16[72,512]{1,0:T(8,128)(2,1)S(1)} %collective-permute-done.2), channel_id=1, source_target_pairs={{0,4},{1,5},{2,6},{3,7},{4,0},{5,1},{6,2},{7,3},{8,12},{9,13},{10,... | collective-permute-start | bytes 221192 | tf_op jit(solution)/shard_map/ppermute | solution.py:187
  15.2 4.4 %collective-permute-start.5 = (bf16[72,512]{1,0:T(8,128)(2,1)S(1)}, bf16[72,512]{1,0:T(8,128)(2,1)S(1)}, u32[]{:S(2)}, u32[]{:S(2)}) collective-permute-start(bf16[72,512]{1,0:T(8,128)(2,1)S(1)} %collective-permute-done.3), channel_id=1, source_target_pairs={{0,4},{1,5},{2,6},{3,7},{4,0},{5,1},{6,2},{7,3},{8,12},{9,13},{10,... | collective-permute-start | bytes 221192 | tf_op jit(solution)/shard_map/ppermute | solution.py:187
  19.6 2.0 %collective-permute-start.6 = (bf16[576,512]{1,0:T(8,128)(2,1)S(1)}, bf16[576,512]{1,0:T(8,128)(2,1)S(1)}, u32[]{:S(2)}, u32[]{:S(2)}) collective-permute-start(bf16[576,512]{1,0:T(8,128)(2,1)S(1)} %constant_dynamic-update-slice_fusion.a_ref), channel_id=1, source_target_pairs={{0,1},{1,0},{2,3},{3,2},{4,5},{5,4},{6,7},{7,6},{8,9},{9,8},{10,11... | collective-permute-start | bytes 1769480 | tf_op jit(solution)/shard_map/ppermute | solution.py:187
  26.5 4.4 %collective-permute-start.7 = (f32[72,256]{1,0:T(8,128)S(1)}, f32[72,256]{1,0:T(8,128)S(1)}, u32[]{:S(2)}, u32[]{:S(2)}) collective-permute-start(f32[72,256]{1,0:T(8,128)S(1)} %get-tuple-element.17), channel_id=1, source_target_pairs={{0,2},{1,3},{2,0},{3,1},{4,6},{5,7},{6,4},{7,5},{8,10},{9,11},{10,... | collective-permute-start | bytes 221192 | tf_op jit(solution)/shard_map/ppermute | solution.py:187

commit v3 on v2

v3 whole, which is shorter than its diff:
```python
import functools
import math

import jax
import jax.numpy as jnp
from jax import lax
from jax.experimental import pallas as pl
from jax.experimental.pallas import tpu as pltpu
from jax.sharding import PartitionSpec as P

HEAD_DIM = 128
TEXT_SLOTS = 512
GATHER_ALL_ROWS = 2048
MASKED = -1e30
ROW_CHUNK = 256
SHARP = math.log2(math.e) / math.sqrt(HEAD_DIM)
VMEM = pl.BlockSpec(memory_space=pltpu.VMEM)
SMEM = pl.BlockSpec(memory_space=pltpu.SMEM)
HBM = pl.BlockSpec(memory_space=pltpu.HBM)


def masked_softmax(scores, key_valid):
    masked = jnp.where(key_valid, scores, -jnp.inf)
    highest = jnp.max(masked, axis=-1, keepdims=True)
    powers = jnp.where(key_valid, jnp.exp(scores - highest), 0.0)
    totals = jnp.sum(powers, axis=-1, keepdims=True)
    return powers / totals


def local_by_rows(query_source, key_source, query_edit, key_edit, text_count):
    local_rows, full_width = query_source.shape
    head_count = full_width // HEAD_DIM
    all_rows = local_rows * lax.axis_size("ctx")
    text_slots = min(TEXT_SLOTS, all_rows // 4)
    score_scale = 1.0 / math.sqrt(HEAD_DIM)
    weight = 4.0 * all_rows * math.sqrt(all_rows)
    places = jnp.arange(all_rows)
    token_valid = (places >= text_slots) | (places < text_count[0])
    own_places = lax.axis_index("ctx") * local_rows + jnp.arange(local_rows)
    own_valid = (own_places >= text_slots) | (own_places < text_count[0])
    own_weight = own_valid.astype(jnp.float32)

    def heads_view(matrix):
        return matrix.reshape(matrix.shape[0], head_count, HEAD_DIM)

    every_ks = lax.all_gather(key_source, "ctx", axis=0, tiled=True)
    every_ke = lax.all_gather(key_edit, "ctx", axis=0, tiled=True)
    own_qs, own_qe = heads_view(query_source), heads_view(query_edit)
    dot = functools.partial(jnp.einsum, preferred_element_type=jnp.float32)
    scores_source = dot("rhd,lhd->hrl", own_qs, heads_view(every_ks)) * score_scale
    scores_edit = dot("rhd,lhd->hrl", own_qe, heads_view(every_ke)) * score_scale
    probs_source = masked_softmax(scores_source, token_valid[None, None, :])
    probs_edit = masked_softmax(scores_edit, token_valid[None, None, :])
    map_grad = 2.0 * weight * (probs_edit - probs_source) * own_weight[None, :, None]
    row_delta = jnp.sum(map_grad * probs_edit, axis=-1, keepdims=True)
    score_grad = (probs_edit * (map_grad - row_delta)).astype(jnp.bfloat16)
    query_grad = dot("hrl,lhd->rhd", score_grad, heads_view(every_ke)) * score_scale
    term_block = dot("hrl,rhd->lhd", score_grad, own_qe) * score_scale
    key_grad = lax.psum_scatter(
        term_block.reshape(all_rows, full_width), "ctx", scatter_dimension=0, tiled=True
    )
    return (query_grad.reshape(local_rows, full_width), key_grad)


def pack_kernel(qs_ref, ks_ref, qe_ref, ke_ref, own_ref, other_ref, held_ref, sems):
    copies = [
        pltpu.make_async_copy(ref, held_ref.at[place], sems.at[place])
        for place, ref in enumerate((qs_ref, ks_ref, qe_ref, ke_ref))
    ]
    for copy in copies:
        copy.start()
    first = (lax.axis_index("ctx") >> 1) & 1 == 0
    for place, copy in enumerate(copies):
        copy.wait()
        low, high = held_ref[place, :, :HEAD_DIM], held_ref[place, :, HEAD_DIM:]
        columns = slice(place * HEAD_DIM, (place + 1) * HEAD_DIM)
        own_ref[:, columns] = jnp.where(first, low, high)
        other_ref[:, columns] = jnp.where(first, high, low)


def mask_kernel(own_rows, text_slots, count_ref, bias_ref, live_ref, live_own_ref):
    me = lax.axis_index("ctx")
    mine = 2 * own_rows
    blocks = bias_ref.shape[0] // mine
    lanes = lax.broadcasted_iota(jnp.int32, live_ref.shape, 1)
    lane_place = lanes
    for k in range(blocks):
        device = me ^ (k // (blocks // 2)) ^ (k % (blocks // 2) * 4)
        first, second = device * own_rows, (device ^ 2) * own_rows - own_rows
        row = lax.broadcasted_iota(jnp.int32, (mine, HEAD_DIM), 0)
        place = jnp.where(row < own_rows, first, second) + row
        live = (place >= text_slots) | (place < count_ref[0])
        bias_ref[k * mine : (k + 1) * mine] = jnp.where(live, 0.0, MASKED).astype(jnp.bfloat16)
        if k == 0:
            live_own_ref[...] = live[:, :1].astype(jnp.float32)
        lane_place = jnp.where(lanes >= k * mine, first + lanes - k * mine, lane_place)
        lane_place = jnp.where(lanes >= k * mine + own_rows, second + lanes - k * mine, lane_place)
    live_ref[...] = ((lane_place >= text_slots) | (lane_place < count_ref[0])).astype(jnp.float32)


def dot_nt(a, b):
    return lax.dot_general(a, b, (((1,), (1,)), ((), ())), preferred_element_type=jnp.float32)


def fold(block, op):
    parts = [block[i : i + 8] for i in range(0, block.shape[0], 8)]
    while len(parts) > 1:
        parts = [op(*parts[i : i + 2]) if i + 1 < len(parts) else parts[i] for i in range(0, len(parts), 2)]
    return parts[0]


def part(refs, which, start, size):
    half = refs[0].shape[0]
    columns = slice(which * HEAD_DIM, (which + 1) * HEAD_DIM)
    if start + size <= half:
        return refs[0][start : start + size, columns]
    if start >= half:
        return refs[1][start - half : start - half + size, columns]
    return jnp.concatenate([refs[0][start:, columns], refs[1][: start + size - half, columns]], axis=0)


def queries(refs, which, start, size):
    one = (lax.broadcasted_iota(jnp.int32, (size, HEAD_DIM), 1) == 0).astype(jnp.bfloat16)
    return jnp.concatenate([part(refs, which, start, size), one], axis=1)


def keys(refs, bias_ref, which, start, size):
    return jnp.concatenate([part(refs, which, start, size), bias_ref[start : start + size]], axis=1)


def row_sums(items, refs, bias_ref, scores_ref, powers_ref, strip):
    half = refs[0].shape[0]

    def score(n):
        start, size, low, high = items[n]
        tops = []
        for m, which in enumerate((0, 2)):
            wide = queries(refs, which, start, size)
            top = None
            for k in range(low, high, half):
                block = dot_nt(keys(refs, bias_ref, which + 1, k, half), wide)
                scores_ref[n % 2, m, k : k + half, :size] = block
                highest = fold(block, jnp.maximum)
                top = highest if top is None else jnp.maximum(top, highest)
            tops.append(jnp.max(top, axis=0, keepdims=True))
        return tops

    tops = score(0)
    for n, (start, size, low, high) in enumerate(items):
        later = score(n + 1) if n + 1 < len(items) else None
        sums = [None] * 4
        for k in range(low, high, strip):
            source, edit = (
                jnp.exp2((scores_ref[n % 2, m, k : k + strip, :size] - tops[m]) * SHARP) for m in range(2)
            )
            if k == 0:
                powers_ref[0, :, start : start + size] = source
                powers_ref[1, :, start : start + size] = edit
            terms = [fold(t, jnp.add) for t in (source, edit, edit * edit, source * edit)]
            sums = [t if s is None else s + t for s, t in zip(sums, terms)]
        yield tops, [jnp.sum(s, axis=0, keepdims=True) for s in sums]
        tops = later


def row_chunks(start, end):
    return [(at, min(ROW_CHUNK, end - at)) for at in range(start, end, ROW_CHUNK)]


def early_kernel(own_rows, a_ref, bias_ref, stats_out, powers_out, scores_ref):
    half = a_ref.shape[0]
    items = [(start, size, 0, half) for start, size in row_chunks(0, stats_out.shape[1])]
    for (start, size, *_), (tops, sums) in zip(
        items, row_sums(items, (a_ref,), bias_ref, scores_ref, powers_out, 2 * own_rows)
    ):
        for row, value in enumerate(tops + sums):
            stats_out[row : row + 1, start : start + size] = value


def head_kernel(
    weight, own_rows, a_ref, b_ref, bias_ref, live_ref, live_own_ref, stats_ref, early_ref, keep_out, send_out,
    scores_ref, powers_ref,
):
    half = a_ref.shape[0]
    rows = 2 * half
    mine = 2 * own_rows
    scale = 1.0 / math.sqrt(HEAD_DIM)
    refs = (a_ref, b_ref)

    def own_powers(which):
        scores = dot_nt(queries(refs, which, 0, mine), keys(refs, bias_ref, which + 1, 0, rows))
        highest = jnp.max(scores, axis=1, keepdims=True)
        powers = jnp.exp2((scores - highest) * SHARP)
        return powers * (1.0 / jnp.sum(powers, axis=1, keepdims=True))

    probs_source, probs_edit = own_powers(0), own_powers(2)
    map_grad = (probs_edit - probs_source) * (2.0 * weight * live_own_ref[...])
    row_delta = jnp.sum(map_grad * probs_edit, axis=1, keepdims=True)
    grad = (probs_edit * (map_grad - row_delta)).astype(jnp.bfloat16)
    query_grad = jnp.dot(grad, part(refs, 3, 0, rows), preferred_element_type=jnp.float32) * scale

    ready = stats_ref.shape[1]
    items = [(start, size, half, rows) for start, size in row_chunks(0, ready)]
    items += [(start, size, 0, rows) for start, size in row_chunks(ready, rows)]
    total = jnp.zeros((mine, HEAD_DIM), jnp.float32)
    for (start, size, low, _), (tops, sums) in zip(
        items, row_sums(items, refs, bias_ref, scores_ref, powers_ref, mine)
    ):
        lanes = slice(start, start + size)
        if low:
            before = [stats_ref[row : row + 1, lanes] for row in range(6)]
            highest = [jnp.maximum(x, y) for x, y in zip(before, tops)]
            old, new = (
                [jnp.exp2((x - y) * SHARP) for x, y in zip(part_tops, highest)] for part_tops in (before, tops)
            )
            sums = [
                x * (old[p] * old[q] if q else old[p]) + y * (new[p] * new[q] if q else new[p])
                for x, y, p, q in zip(before[2:], sums, (0, 1, 1, 0), (0, 0, 1, 1))
            ]
            powers_source, powers_edit = early_ref[0, :, lanes] * old[0], early_ref[1, :, lanes] * old[1]
        else:
            powers_source, powers_edit = powers_ref[0, :, lanes], powers_ref[1, :, lanes]
        sum_source, sum_edit, square, cross = sums
        over_source, over_edit = 1.0 / sum_source, 1.0 / sum_edit
        factor = 2.0 * weight * live_ref[:, lanes]
        delta = factor * (square * over_edit - cross * over_source) * over_edit
        probs_edit = powers_edit * over_edit
        probs_source = powers_source * over_source
        grad = (probs_edit * (factor * (probs_edit - probs_source) - delta)).astype(jnp.bfloat16)
        total = total + jnp.dot(grad, part(refs, 2, start, size), preferred_element_type=jnp.float32)
    for columns, grad in ((slice(None, HEAD_DIM), query_grad), (slice(HEAD_DIM, None), total * scale)):
        keep_out[:, columns] = grad[:own_rows]
        send_out[:, columns] = grad[own_rows:].astype(send_out.dtype)


def local_by_heads(query_source, key_source, query_edit, key_edit, text_count):
    local_rows, full_width = query_source.shape
    size = lax.axis_size("ctx")
    all_rows = local_rows * size
    text_slots = min(TEXT_SLOTS, all_rows // 4)
    weight = 4.0 * all_rows * math.sqrt(all_rows)
    me = lax.axis_index("ctx")
    head = (me >> 1) & 1
    arrays = (query_source, key_source, query_edit, key_edit)

    def swap(array, bits):
        return lax.ppermute(array, "ctx", [(i, i ^ bits) for i in range(size)])

    pack = jax.ShapeDtypeStruct((local_rows, 4 * HEAD_DIM), jnp.bfloat16)
    own, other = pl.pallas_call(
        pack_kernel,
        out_shape=(pack, pack),
        in_specs=[HBM] * 4,
        out_specs=(VMEM, VMEM),
        scratch_shapes=[pltpu.VMEM((4, local_rows, full_width), jnp.bfloat16), pltpu.SemaphoreType.DMA((4,))],
        compiler_params=pltpu.CompilerParams(vmem_limit_bytes=4 * 1024 * 1024),
        name="pack",
    )(*(pltpu.with_memory_space_constraint(x, pltpu.HBM) for x in arrays))

    mine = 2 * local_rows
    partner = swap(other, 2)
    two = jnp.concatenate([own, partner], axis=0)
    far = [(0, own), (local_rows, partner)]
    for bit in [1 << p for p in range(size.bit_length() - 2, 2, -1)]:
        far += [(at + bit * mine // 4, swap(block, bit)) for at, block in far]
    far = far[2:]
    blocks = [(0, two), (mine, swap(two, 4))] + far + [(at + mine, swap(block, 4)) for at, block in far]
    held = jnp.concatenate([block for _, block in sorted(blocks, key=lambda entry: entry[0])], axis=0)
    held, count = lax.optimization_barrier((held, text_count))
    across = swap(held, 1)
    bias, live, live_own = pl.pallas_call(
        functools.partial(mask_kernel, local_rows, text_slots),
        out_shape=(
            jax.ShapeDtypeStruct((all_rows, HEAD_DIM), jnp.bfloat16),
            jax.ShapeDtypeStruct((1, all_rows), jnp.float32),
            jax.ShapeDtypeStruct((mine, 1), jnp.float32),
        ),
        in_specs=[SMEM],
        out_specs=(VMEM,) * 3,
        compiler_params=pltpu.CompilerParams(vmem_limit_bytes=4 * 1024 * 1024),
        name="mask",
    )(count)

    half = all_rows // 2
    ready = half // ROW_CHUNK * ROW_CHUNK
    scores = pltpu.VMEM((2, 2, all_rows, ROW_CHUNK), jnp.float32)
    stats, powers = pl.pallas_call(
        functools.partial(early_kernel, local_rows),
        out_shape=(
            jax.ShapeDtypeStruct((8, ready), jnp.float32),
            jax.ShapeDtypeStruct((2, mine, ready), jnp.float32),
        ),
        in_specs=[VMEM] * 2,
        out_specs=(VMEM, VMEM),
        scratch_shapes=[scores],
        compiler_params=pltpu.CompilerParams(vmem_limit_bytes=32 * 1024 * 1024),
        name="early",
    )(held, bias)

    grads = jax.ShapeDtypeStruct((local_rows, 2 * HEAD_DIM), jnp.float32)
    keep, send = pl.pallas_call(
        functools.partial(head_kernel, weight, local_rows),
        out_shape=(grads, grads),
        in_specs=[VMEM] * 7,
        out_specs=(VMEM, VMEM),
        scratch_shapes=[scores, pltpu.VMEM((2, mine, all_rows), jnp.float32)],
        compiler_params=pltpu.CompilerParams(vmem_limit_bytes=40 * 1024 * 1024),
        name="head",
    )(held, across, bias, live, live_own, stats, powers)
    back = swap(send, 2)

    def both_heads(columns):
        mine, other = keep[:, columns], back[:, columns]
        return jnp.where(
            head == 0, jnp.concatenate([mine, other], axis=1), jnp.concatenate([other, mine], axis=1)
        )

    return both_heads(slice(None, HEAD_DIM)), both_heads(slice(HEAD_DIM, None))


def local(query_source, key_source, query_edit, key_edit, text_count):
    local_rows, full_width = query_source.shape
    size = lax.axis_size("ctx")
    small = 2 * ROW_CHUNK <= local_rows * size <= GATHER_ALL_ROWS
    if full_width == 2 * HEAD_DIM and small and size >= 8 and size & (size - 1) == 0 and local_rows % 8 == 0:
        return local_by_heads(query_source, key_source, query_edit, key_edit, text_count)
    return local_by_rows(query_source, key_source, query_edit, key_edit, text_count)


def solution(mesh):
    split = P(("req", "ctx"), None)
    return jax.shard_map(
        local, mesh=mesh, in_specs=(split,) * 4 + (P("req"),), out_specs=(split, split), check_vma=False
    )
```

time: 31.8 us -> 30.9 us (0.972)
  waiting for transfers between devices: 10.2 us -> 8.45 us
  starting transfers between devices: 12.9 us -> 14 us
  Pallas kernels: 5.78 us -> 6.17 us
  local copies, waits for them, and re-layouts: 0.38 us -> 0.06 us
    ppermute x8, waiting for transfers between devices: 10.2 us -> 8.45 us  [swap(): return lax.ppermute(array, 'ctx', [(i, i ^ bits) for i in range(size)])]
    pallas_call x1 -> x3, Pallas kernels: 0.86 us -> 2.03 us  [the longest x1 1.02 us: local_by_heads(): pl.pallas_call(functools.partial(early_kernel, local_rows), out_shape=(ja...]
    ppermute x8, starting transfers between devices: 12.9 us -> 14 us  [swap(): return lax.ppermute(array, 'ctx', [(i, i ^ bits) for i in range(size)])]
    pallas_call x1, Pallas kernels: 4.92 us -> 4.14 us  [local_by_heads(): pl.pallas_call(functools.partial(head_kernel, weight, local_rows), out_sh...]
  transfers between devices with their start and end apart: 8 -> 8, of which waited for: 4 -> 4; matrix products, arithmetic and copies ran while one was open for 2% -> 0% of each run, Pallas kernels for 0% -> 4%
where the time goes in v3:
time: 30.9 us; the launch traced here: 30.7 us
  starting transfers between devices  14 us (45%)
  waiting for transfers between devices  8.45 us (27%)
  Pallas kernels  6.17 us (20%)
  between operations  1.36 us (4%)
  other arithmetic  0.68 us (2%)
    ppermute x8, starting transfers between devices, swap(): return lax.ppermute(array, 'ctx', [(i, i ^ bits) for i in range(size)])  14 us
    ppermute x8, waiting for transfers between devices, swap(): return lax.ppermute(array, 'ctx', [(i, i ^ bits) for i in range(size)])  8.45 us
    pallas_call x1, Pallas kernels, local_by_heads(): pl.pallas_call(functools.partial(head_kernel, weight, local_rows), out_sh...  4.14 us
    pallas_call x1, Pallas kernels, local_by_heads(): pl.pallas_call(functools.partial(early_kernel, local_rows), out_shape=(ja...  1.02 us
    pallas_call x1, Pallas kernels, local_by_heads(): pl.pallas_call(pack_kernel, out_shape=(pack, pack), in_specs=[HBM] * 4, o...  0.86 us
    select_n x1, other arithmetic, both_heads(): jnp.where(head == 0, jnp.concatenate([mine, other], axis=1), jnp.concaten...  0.67 us
  transfers between devices with their start and end apart: 8, of which 4 were waited for; matrix products, arithmetic and copies ran while one was open for 0% of the time, Pallas kernels for 4%

profile of v3, /device:TPU:0, one launch (start us, length us, event | category | flops | bytes accessed | tf_op | source)
XLA Modules:
  0.0 30.7 jit_solution(13589256426202140865)
XLA Ops:
  0.6 0.9 %pack.1 = (bf16[72,512]{1,0:T(8,128)(2,1)S(1)}, bf16[72,512]{1,0:T(8,128)(2,1)S(1)}) custom-call(bf16[72,256]{1,0:T(8,128)(2,1)} %qs_ref.1, bf16[72,256]{1,0:T(8,128)(2,1)} %ks_ref.1, bf16[72,256]{1,0:T(8,128)(2,1)} %qe_ref.1, bf16[72,256]{1,0:T(8,128)(2,1)} %ke_ref.1), custom_call_target="tpu_custom_call" | custom-call | tf_op jit(solution)/shard_map/pack/pallas_call | solution.py:249
  1.5 3.0 %collective-permute-start = (bf16[72,512]{1,0:T(8,128)(2,1)S(1)}, bf16[72,512]{1,0:T(8,128)(2,1)S(1)}, u32[]{:S(2)}, u32[]{:S(2)}) collective-permute-start(bf16[72,512]{1,0:T(8,128)(2,1)S(1)} %get-tuple-element.14), channel_id=1, source_target_pairs={{0,2},{1,3},{2,0},{3,1},{4,6},{5,7},{6,4},{7,5},{8,10},{9,11},{10,... | collective-permute-start | bytes 221192 | tf_op jit(solution)/shard_map/ppermute | solution.py:246
  4.5 2.6 %collective-permute-start.2 = (bf16[72,512]{1,0:T(8,128)(2,1)S(1)}, bf16[72,512]{1,0:T(8,128)(2,1)S(1)}, u32[]{:S(2)}, u32[]{:S(2)}) collective-permute-start(bf16[72,512]{1,0:T(8,128)(2,1)S(1)} %get-tuple-element.13), channel_id=1, source_target_pairs={{0,8},{1,9},{2,10},{3,11},{4,12},{5,13},{6,14},{7,15},{8,0},{9,1},... | collective-permute-start | bytes 221192 | tf_op jit(solution)/shard_map/ppermute | solution.py:246
  7.1 0.0 collective-permute-done
  7.1 1.9 %collective-permute-start.1 = (bf16[144,512]{1,0:T(8,128)(2,1)S(1)}, bf16[144,512]{1,0:T(8,128)(2,1)S(1)}, u32[]{:S(2)}, u32[]{:S(2)}) collective-permute-start(bf16[144,512]{1,0:T(8,128)(2,1)S(1)} %pad_maximum_fusion), channel_id=1, source_target_pairs={{0,4},{1,5},{2,6},{3,7},{4,0},{5,1},{6,2},{7,3},{8,12},{9,13},{10,... | collective-permute-start | bytes 442376 | tf_op jit(solution)/shard_map/ppermute | solution.py:246
  9.0 2.6 %collective-permute-start.3 = (bf16[72,512]{1,0:T(8,128)(2,1)S(1)}, bf16[72,512]{1,0:T(8,128)(2,1)S(1)}, u32[]{:S(2)}, u32[]{:S(2)}) collective-permute-start(bf16[72,512]{1,0:T(8,128)(2,1)S(1)} %collective-permute-done), channel_id=1, source_target_pairs={{0,8},{1,9},{2,10},{3,11},{4,12},{5,13},{6,14},{7,15},{8,0},{9,1},... | collective-permute-start | bytes 221192 | tf_op jit(solution)/shard_map/ppermute | solution.py:246
  11.6 0.0 collective-permute-done.2
  11.6 0.5 %collective-permute-start.4 = (bf16[72,512]{1,0:T(8,128)(2,1)S(1)}, bf16[72,512]{1,0:T(8,128)(2,1)S(1)}, u32[]{:S(2)}, u32[]{:S(2)}) collective-permute-start(bf16[72,512]{1,0:T(8,128)(2,1)S(1)} %collective-permute-done.2), channel_id=1, source_target_pairs={{0,4},{1,5},{2,6},{3,7},{4,0},{5,1},{6,2},{7,3},{8,12},{9,13},{10,... | collective-permute-start | bytes 221192 | tf_op jit(solution)/shard_map/ppermute | solution.py:246
  12.1 2.8 %collective-permute-done.3 = bf16[72,512]{1,0:T(8,128)(2,1)S(1)} collective-permute-done((bf16[72,512]{1,0:T(8,128)(2,1)S(1)}, bf16[72,512]{1,0:T(8,128)(2,1)S(1)}, u32[]{:S(2)}, u32[]{:S(2)}) %collective-permute-start.3) | collective-permute-done | bytes 73760 | tf_op jit(solution)/shard_map/ppermute | solution.py:246
  14.9 2.0 %collective-permute-start.5 = (bf16[72,512]{1,0:T(8,128)(2,1)S(1)}, bf16[72,512]{1,0:T(8,128)(2,1)S(1)}, u32[]{:S(2)}, u32[]{:S(2)}) collective-permute-start(bf16[72,512]{1,0:T(8,128)(2,1)S(1)} %collective-permute-done.3), channel_id=1, source_target_pairs={{0,4},{1,5},{2,6},{3,7},{4,0},{5,1},{6,2},{7,3},{8,12},{9,13},{10,... | collective-permute-start | bytes 221192 | tf_op jit(solution)/shard_map/ppermute | solution.py:246
  16.9 0.0 collective-permute-done.1
  16.9 0.0 collective-permute-done.4
  16.9 2.3 %collective-permute-done.5 = bf16[72,512]{1,0:T(8,128)(2,1)S(1)} collective-permute-done((bf16[72,512]{1,0:T(8,128)(2,1)S(1)}, bf16[72,512]{1,0:T(8,128)(2,1)S(1)}, u32[]{:S(2)}, u32[]{:S(2)}) %collective-permute-start.5) | collective-permute-done | bytes 73760 | tf_op jit(solution)/shard_map/ppermute | solution.py:246
  19.3 0.0 collective-permute-start.6
  19.9 0.1 mask.1
  20.1 1.0 %early.1 = (f32[8,512]{1,0:T(8,128)S(1)}, f32[2,144,512]{2,1,0:T(8,128)S(1)}) custom-call(bf16[576,512]{1,0:T(8,128)(2,1)S(1)} %constant_dynamic-update-slice_fusion.a_ref, bf16[1152,128]{1,0:T(8,128)(2,1)S(1)} %get-tuple-element.17.bias_ref), custom_call_target="tpu_custom_call" | custom-call | tf_op jit(solution)/shard_map/early/pallas_call | solution.py:286
  21.1 0.2 collective-permute-done.6.b_ref
  21.3 4.1 %head.1 = (f32[72,256]{1,0:T(8,128)S(1)}, f32[72,256]{1,0:T(8,128)S(1)}) custom-call(bf16[576,512]{1,0:T(8,128)(2,1)S(1)} %constant_dynamic-update-slice_fusion.a_ref, bf16[576,512]{1,0:T(8,128)(2,1)S(1)} %collective-permute-done.6.b_ref, bf16[1152,128]{1,0:T(8,128)(2,1)S(1)} %get-tuple-element.17.bias_ref, f32[1,1152]{1,0:T(1,128)S(1)} %get-tuple-element.18.live_ref, ...), custom_call_target="tpu_custom_call" | custom-call | tf_op jit(solution)/shard_map/head/pallas_call | solution.py:300
  25.4 1.5 %collective-permute-start.7 = (f32[72,256]{1,0:T(8,128)S(1)}, f32[72,256]{1,0:T(8,128)S(1)}, u32[]{:S(2)}, u32[]{:S(2)}) collective-permute-start(f32[72,256]{1,0:T(8,128)S(1)} %get-tuple-element.23), channel_id=1, source_target_pairs={{0,2},{1,3},{2,0},{3,1},{4,6},{5,7},{6,4},{7,5},{8,10},{9,11},{10,... | collective-permute-start | bytes 221192 | tf_op jit(solution)/shard_map/ppermute | solution.py:246
  26.9 3.1 %collective-permute-done.7 = f32[72,256]{1,0:T(8,128)S(1)} collective-permute-done((f32[72,256]{1,0:T(8,128)S(1)}, f32[72,256]{1,0:T(8,128)S(1)}, u32[]{:S(2)}, u32[]{:S(2)}) %collective-permute-start.7) | collective-permute-done | bytes 73760 | tf_op jit(solution)/shard_map/ppermute | solution.py:246
  30.0 0.7 %maximum_select_fusion = (f32[72,256]{1,0:T(8,128)}, f32[72,256]{1,0:T(8,128)}) fusion(f32[72,128]{1,0:T(8,128)S(1)} %get-tuple-element.27, f32[72,128]{1,0:T(8,128)S(1)} %get-tuple-element.25, pred[]{:T(512)S(6)} %eq.4, f32[72,128]{1,0:T(8,128)S(1)} %get-tuple-element.24, f32[72,128]{1,0:T(8,128)S(1)} %get-tuple-element.26), kind=kLoop, calls=%fused_computation.1 | loop fusion | flops 110592 | bytes 294913 | tf_op jit(solution)/shard_map/jit(_where)/select_n | solution.py:313
  (10 shorter events, 0.1 us)
Async XLA Ops:
  1.5 5.6 %collective-permute-start = (bf16[72,512]{1,0:T(8,128)(2,1)S(1)}, bf16[72,512]{1,0:T(8,128)(2,1)S(1)}, u32[]{:S(2)}, u32[]{:S(2)}) collective-permute-start(bf16[72,512]{1,0:T(8,128)(2,1)S(1)} %get-tuple-element.14), channel_id=1, source_target_pairs={{0,2},{1,3},{2,0},{3,1},{4,6},{5,7},{6,4},{7,5},{8,10},{9,11},{10,... | collective-permute-start | bytes 221192 | tf_op jit(solution)/shard_map/ppermute | solution.py:246
  4.5 7.1 %collective-permute-start.2 = (bf16[72,512]{1,0:T(8,128)(2,1)S(1)}, bf16[72,512]{1,0:T(8,128)(2,1)S(1)}, u32[]{:S(2)}, u32[]{:S(2)}) collective-permute-start(bf16[72,512]{1,0:T(8,128)(2,1)S(1)} %get-tuple-element.13), channel_id=1, source_target_pairs={{0,8},{1,9},{2,10},{3,11},{4,12},{5,13},{6,14},{7,15},{8,0},{9,1},... | collective-permute-start | bytes 221192 | tf_op jit(solution)/shard_map/ppermute | solution.py:246
  7.1 9.8 %collective-permute-start.1 = (bf16[144,512]{1,0:T(8,128)(2,1)S(1)}, bf16[144,512]{1,0:T(8,128)(2,1)S(1)}, u32[]{:S(2)}, u32[]{:S(2)}) collective-permute-start(bf16[144,512]{1,0:T(8,128)(2,1)S(1)} %pad_maximum_fusion), channel_id=1, source_target_pairs={{0,4},{1,5},{2,6},{3,7},{4,0},{5,1},{6,2},{7,3},{8,12},{9,13},{10,... | collective-permute-start | bytes 442376 | tf_op jit(solution)/shard_map/ppermute | solution.py:246
  9.0 5.9 %collective-permute-start.3 = (bf16[72,512]{1,0:T(8,128)(2,1)S(1)}, bf16[72,512]{1,0:T(8,128)(2,1)S(1)}, u32[]{:S(2)}, u32[]{:S(2)}) collective-permute-start(bf16[72,512]{1,0:T(8,128)(2,1)S(1)} %collective-permute-done), channel_id=1, source_target_pairs={{0,8},{1,9},{2,10},{3,11},{4,12},{5,13},{6,14},{7,15},{8,0},{9,1},... | collective-permute-start | bytes 221192 | tf_op jit(solution)/shard_map/ppermute | solution.py:246
  11.6 5.3 %collective-permute-start.4 = (bf16[72,512]{1,0:T(8,128)(2,1)S(1)}, bf16[72,512]{1,0:T(8,128)(2,1)S(1)}, u32[]{:S(2)}, u32[]{:S(2)}) collective-permute-start(bf16[72,512]{1,0:T(8,128)(2,1)S(1)} %collective-permute-done.2), channel_id=1, source_target_pairs={{0,4},{1,5},{2,6},{3,7},{4,0},{5,1},{6,2},{7,3},{8,12},{9,13},{10,... | collective-permute-start | bytes 221192 | tf_op jit(solution)/shard_map/ppermute | solution.py:246
  14.9 4.4 %collective-permute-start.5 = (bf16[72,512]{1,0:T(8,128)(2,1)S(1)}, bf16[72,512]{1,0:T(8,128)(2,1)S(1)}, u32[]{:S(2)}, u32[]{:S(2)}) collective-permute-start(bf16[72,512]{1,0:T(8,128)(2,1)S(1)} %collective-permute-done.3), channel_id=1, source_target_pairs={{0,4},{1,5},{2,6},{3,7},{4,0},{5,1},{6,2},{7,3},{8,12},{9,13},{10,... | collective-permute-start | bytes 221192 | tf_op jit(solution)/shard_map/ppermute | solution.py:246
  19.3 2.0 %collective-permute-start.6 = (bf16[576,512]{1,0:T(8,128)(2,1)S(1)}, bf16[576,512]{1,0:T(8,128)(2,1)S(1)}, u32[]{:S(2)}, u32[]{:S(2)}) collective-permute-start(bf16[576,512]{1,0:T(8,128)(2,1)S(1)} %constant_dynamic-update-slice_fusion.a_ref), channel_id=1, source_target_pairs={{0,1},{1,0},{2,3},{3,2},{4,5},{5,4},{6,7},{7,6},{8,9},{9,8},{10,11... | collective-permute-start | bytes 1769480 | tf_op jit(solution)/shard_map/ppermute | solution.py:246
  25.4 4.6 %collective-permute-start.7 = (f32[72,256]{1,0:T(8,128)S(1)}, f32[72,256]{1,0:T(8,128)S(1)}, u32[]{:S(2)}, u32[]{:S(2)}) collective-permute-start(f32[72,256]{1,0:T(8,128)S(1)} %get-tuple-element.23), channel_id=1, source_target_pairs={{0,2},{1,3},{2,0},{3,1},{4,6},{5,7},{6,4},{7,5},{8,10},{9,11},{10,... | collective-permute-start | bytes 221192 | tf_op jit(solution)/shard_map/ppermute | solution.py:246

commit v4 on v3

--- a/solution.py
+++ b/solution.py
@@ -299,7 +299,7 @@
     grads = jax.ShapeDtypeStruct((local_rows, 2 * HEAD_DIM), jnp.float32)
     keep, send = pl.pallas_call(
         functools.partial(head_kernel, weight, local_rows),
-        out_shape=(grads, grads),
+        out_shape=(grads, jax.ShapeDtypeStruct(grads.shape, jnp.bfloat16)),
         in_specs=[VMEM] * 7,
         out_specs=(VMEM, VMEM),
         scratch_shapes=[scores, pltpu.VMEM((2, mine, all_rows), jnp.float32)],
@@ -309,7 +309,7 @@
     back = swap(send, 2)
 
     def both_heads(columns):
-        mine, other = keep[:, columns], back[:, columns]
+        mine, other = keep[:, columns], back[:, columns].astype(jnp.float32)
         return jnp.where(
             head == 0, jnp.concatenate([mine, other], axis=1), jnp.concatenate([other, mine], axis=1)
         )

time: 30.9 us -> 30.3 us (0.981)
  waiting for transfers between devices: 8.45 us -> 7.88 us
    ppermute x8, waiting for transfers between devices: 8.45 us -> 7.88 us  [swap(): return lax.ppermute(array, 'ctx', [(i, i ^ bits) for i in range(size)])]
where the time goes in v4:
time: 30.3 us; the launch traced here: 30.1 us
  starting transfers between devices  14 us (46%)
  waiting for transfers between devices  7.88 us (26%)
  Pallas kernels  6.17 us (20%)
  between operations  1.36 us (4%)
  other arithmetic  0.69 us (2%)
    ppermute x8, starting transfers between devices, swap(): return lax.ppermute(array, 'ctx', [(i, i ^ bits) for i in range(size)])  14 us
    ppermute x8, waiting for transfers between devices, swap(): return lax.ppermute(array, 'ctx', [(i, i ^ bits) for i in range(size)])  7.88 us
    pallas_call x1, Pallas kernels, local_by_heads(): pl.pallas_call(functools.partial(head_kernel, weight, local_rows), out_sh...  4.14 us
    pallas_call x1, Pallas kernels, local_by_heads(): pl.pallas_call(functools.partial(early_kernel, local_rows), out_shape=(ja...  1.02 us
    pallas_call x1, Pallas kernels, local_by_heads(): pl.pallas_call(pack_kernel, out_shape=(pack, pack), in_specs=[HBM] * 4, o...  0.86 us
    select_n x1, other arithmetic, both_heads(): jnp.where(head == 0, jnp.concatenate([mine, other], axis=1), jnp.concaten...  0.67 us
  transfers between devices with their start and end apart: 8, of which 4 were waited for; matrix products, arithmetic and copies ran while one was open for 0% of the time, Pallas kernels for 4%

profile of v4, /device:TPU:0, one launch (start us, length us, event | category | flops | bytes accessed | tf_op | source)
XLA Modules:
  0.0 30.1 jit_solution(3328165130012498154)
XLA Ops:
  0.6 0.9 %pack.1 = (bf16[72,512]{1,0:T(8,128)(2,1)S(1)}, bf16[72,512]{1,0:T(8,128)(2,1)S(1)}) custom-call(bf16[72,256]{1,0:T(8,128)(2,1)} %qs_ref.1, bf16[72,256]{1,0:T(8,128)(2,1)} %ks_ref.1, bf16[72,256]{1,0:T(8,128)(2,1)} %qe_ref.1, bf16[72,256]{1,0:T(8,128)(2,1)} %ke_ref.1), custom_call_target="tpu_custom_call" | custom-call | tf_op jit(solution)/shard_map/pack/pallas_call | solution.py:249
  1.5 3.0 %collective-permute-start = (bf16[72,512]{1,0:T(8,128)(2,1)S(1)}, bf16[72,512]{1,0:T(8,128)(2,1)S(1)}, u32[]{:S(2)}, u32[]{:S(2)}) collective-permute-start(bf16[72,512]{1,0:T(8,128)(2,1)S(1)} %get-tuple-element.14), channel_id=1, source_target_pairs={{0,2},{1,3},{2,0},{3,1},{4,6},{5,7},{6,4},{7,5},{8,10},{9,11},{10,... | collective-permute-start | bytes 221192 | tf_op jit(solution)/shard_map/ppermute | solution.py:246
  4.5 2.6 %collective-permute-start.2 = (bf16[72,512]{1,0:T(8,128)(2,1)S(1)}, bf16[72,512]{1,0:T(8,128)(2,1)S(1)}, u32[]{:S(2)}, u32[]{:S(2)}) collective-permute-start(bf16[72,512]{1,0:T(8,128)(2,1)S(1)} %get-tuple-element.13), channel_id=1, source_target_pairs={{0,8},{1,9},{2,10},{3,11},{4,12},{5,13},{6,14},{7,15},{8,0},{9,1},... | collective-permute-start | bytes 221192 | tf_op jit(solution)/shard_map/ppermute | solution.py:246
  7.1 0.0 collective-permute-done
  7.1 1.9 %collective-permute-start.1 = (bf16[144,512]{1,0:T(8,128)(2,1)S(1)}, bf16[144,512]{1,0:T(8,128)(2,1)S(1)}, u32[]{:S(2)}, u32[]{:S(2)}) collective-permute-start(bf16[144,512]{1,0:T(8,128)(2,1)S(1)} %pad_maximum_fusion), channel_id=1, source_target_pairs={{0,4},{1,5},{2,6},{3,7},{4,0},{5,1},{6,2},{7,3},{8,12},{9,13},{10,... | collective-permute-start | bytes 442376 | tf_op jit(solution)/shard_map/ppermute | solution.py:246
  9.0 2.6 %collective-permute-start.3 = (bf16[72,512]{1,0:T(8,128)(2,1)S(1)}, bf16[72,512]{1,0:T(8,128)(2,1)S(1)}, u32[]{:S(2)}, u32[]{:S(2)}) collective-permute-start(bf16[72,512]{1,0:T(8,128)(2,1)S(1)} %collective-permute-done), channel_id=1, source_target_pairs={{0,8},{1,9},{2,10},{3,11},{4,12},{5,13},{6,14},{7,15},{8,0},{9,1},... | collective-permute-start | bytes 221192 | tf_op jit(solution)/shard_map/ppermute | solution.py:246
  11.6 0.0 collective-permute-done.2
  11.6 0.5 %collective-permute-start.4 = (bf16[72,512]{1,0:T(8,128)(2,1)S(1)}, bf16[72,512]{1,0:T(8,128)(2,1)S(1)}, u32[]{:S(2)}, u32[]{:S(2)}) collective-permute-start(bf16[72,512]{1,0:T(8,128)(2,1)S(1)} %collective-permute-done.2), channel_id=1, source_target_pairs={{0,4},{1,5},{2,6},{3,7},{4,0},{5,1},{6,2},{7,3},{8,12},{9,13},{10,... | collective-permute-start | bytes 221192 | tf_op jit(solution)/shard_map/ppermute | solution.py:246
  12.1 2.8 %collective-permute-done.3 = bf16[72,512]{1,0:T(8,128)(2,1)S(1)} collective-permute-done((bf16[72,512]{1,0:T(8,128)(2,1)S(1)}, bf16[72,512]{1,0:T(8,128)(2,1)S(1)}, u32[]{:S(2)}, u32[]{:S(2)}) %collective-permute-start.3) | collective-permute-done | bytes 73760 | tf_op jit(solution)/shard_map/ppermute | solution.py:246
  14.9 2.0 %collective-permute-start.5 = (bf16[72,512]{1,0:T(8,128)(2,1)S(1)}, bf16[72,512]{1,0:T(8,128)(2,1)S(1)}, u32[]{:S(2)}, u32[]{:S(2)}) collective-permute-start(bf16[72,512]{1,0:T(8,128)(2,1)S(1)} %collective-permute-done.3), channel_id=1, source_target_pairs={{0,4},{1,5},{2,6},{3,7},{4,0},{5,1},{6,2},{7,3},{8,12},{9,13},{10,... | collective-permute-start | bytes 221192 | tf_op jit(solution)/shard_map/ppermute | solution.py:246
  16.9 0.0 collective-permute-done.1
  16.9 0.0 collective-permute-done.4
  16.9 2.3 %collective-permute-done.5 = bf16[72,512]{1,0:T(8,128)(2,1)S(1)} collective-permute-done((bf16[72,512]{1,0:T(8,128)(2,1)S(1)}, bf16[72,512]{1,0:T(8,128)(2,1)S(1)}, u32[]{:S(2)}, u32[]{:S(2)}) %collective-permute-start.5) | collective-permute-done | bytes 73760 | tf_op jit(solution)/shard_map/ppermute | solution.py:246
  19.3 0.0 collective-permute-start.6
  19.9 0.1 mask.1
  20.1 1.0 %early.1 = (f32[8,512]{1,0:T(8,128)S(1)}, f32[2,144,512]{2,1,0:T(8,128)S(1)}) custom-call(bf16[576,512]{1,0:T(8,128)(2,1)S(1)} %constant_dynamic-update-slice_fusion.a_ref, bf16[1152,128]{1,0:T(8,128)(2,1)S(1)} %get-tuple-element.17.bias_ref), custom_call_target="tpu_custom_call" | custom-call | tf_op jit(solution)/shard_map/early/pallas_call | solution.py:286
  21.1 0.2 collective-permute-done.6.b_ref
  21.3 4.1 %head.1 = (f32[72,256]{1,0:T(8,128)S(1)}, bf16[72,256]{1,0:T(8,128)(2,1)S(1)}) custom-call(bf16[576,512]{1,0:T(8,128)(2,1)S(1)} %constant_dynamic-update-slice_fusion.a_ref, bf16[576,512]{1,0:T(8,128)(2,1)S(1)} %collective-permute-done.6.b_ref, bf16[1152,128]{1,0:T(8,128)(2,1)S(1)} %get-tuple-element.17.bias_ref, f32[1,1152]{1,0:T(1,128)S(1)} %get-tuple-element.18.live_ref, ...), custom_call_target="tpu_custom_call" | custom-call | tf_op jit(solution)/shard_map/head/pallas_call | solution.py:300
  25.4 1.5 %collective-permute-start.7 = (bf16[72,256]{1,0:T(8,128)(2,1)S(1)}, bf16[72,256]{1,0:T(8,128)(2,1)S(1)}, u32[]{:S(2)}, u32[]{:S(2)}) collective-permute-start(bf16[72,256]{1,0:T(8,128)(2,1)S(1)} %get-tuple-element.23), channel_id=1, source_target_pairs={{0,2},{1,3},{2,0},{3,1},{4,6},{5,7},{6,4},{7,5},{8,10},{9,11},{10,... | collective-permute-start | bytes 110600 | tf_op jit(solution)/shard_map/ppermute | solution.py:246
  26.9 2.5 %collective-permute-done.7 = bf16[72,256]{1,0:T(8,128)(2,1)S(1)} collective-permute-done((bf16[72,256]{1,0:T(8,128)(2,1)S(1)}, bf16[72,256]{1,0:T(8,128)(2,1)S(1)}, u32[]{:S(2)}, u32[]{:S(2)}) %collective-permute-start.7) | collective-permute-done | bytes 36896 | tf_op jit(solution)/shard_map/ppermute | solution.py:246
  29.5 0.7 %maximum_select_fusion = (f32[72,256]{1,0:T(8,128)}, f32[72,256]{1,0:T(8,128)}) fusion(f32[72,128]{1,0:T(8,128)S(1)} %get-tuple-element.27, f32[72,128]{1,0:T(8,128)S(1)} %get-tuple-element.25, pred[]{:T(512)S(6)} %eq.4, f32[72,128]{1,0:T(8,128)S(1)} %get-tuple-element.24, f32[72,128]{1,0:T(8,128)S(1)} %get-tuple-element.26), kind=kLoop, calls=%fused_computation.1 | loop fusion | flops 110592 | bytes 294913 | tf_op jit(solution)/shard_map/jit(_where)/select_n | solution.py:313
  (10 shorter events, 0.1 us)
Async XLA Ops:
  1.5 5.6 %collective-permute-start = (bf16[72,512]{1,0:T(8,128)(2,1)S(1)}, bf16[72,512]{1,0:T(8,128)(2,1)S(1)}, u32[]{:S(2)}, u32[]{:S(2)}) collective-permute-start(bf16[72,512]{1,0:T(8,128)(2,1)S(1)} %get-tuple-element.14), channel_id=1, source_target_pairs={{0,2},{1,3},{2,0},{3,1},{4,6},{5,7},{6,4},{7,5},{8,10},{9,11},{10,... | collective-permute-start | bytes 221192 | tf_op jit(solution)/shard_map/ppermute | solution.py:246
  4.5 7.1 %collective-permute-start.2 = (bf16[72,512]{1,0:T(8,128)(2,1)S(1)}, bf16[72,512]{1,0:T(8,128)(2,1)S(1)}, u32[]{:S(2)}, u32[]{:S(2)}) collective-permute-start(bf16[72,512]{1,0:T(8,128)(2,1)S(1)} %get-tuple-element.13), channel_id=1, source_target_pairs={{0,8},{1,9},{2,10},{3,11},{4,12},{5,13},{6,14},{7,15},{8,0},{9,1},... | collective-permute-start | bytes 221192 | tf_op jit(solution)/shard_map/ppermute | solution.py:246
  7.1 9.8 %collective-permute-start.1 = (bf16[144,512]{1,0:T(8,128)(2,1)S(1)}, bf16[144,512]{1,0:T(8,128)(2,1)S(1)}, u32[]{:S(2)}, u32[]{:S(2)}) collective-permute-start(bf16[144,512]{1,0:T(8,128)(2,1)S(1)} %pad_maximum_fusion), channel_id=1, source_target_pairs={{0,4},{1,5},{2,6},{3,7},{4,0},{5,1},{6,2},{7,3},{8,12},{9,13},{10,... | collective-permute-start | bytes 442376 | tf_op jit(solution)/shard_map/ppermute | solution.py:246
  9.0 5.9 %collective-permute-start.3 = (bf16[72,512]{1,0:T(8,128)(2,1)S(1)}, bf16[72,512]{1,0:T(8,128)(2,1)S(1)}, u32[]{:S(2)}, u32[]{:S(2)}) collective-permute-start(bf16[72,512]{1,0:T(8,128)(2,1)S(1)} %collective-permute-done), channel_id=1, source_target_pairs={{0,8},{1,9},{2,10},{3,11},{4,12},{5,13},{6,14},{7,15},{8,0},{9,1},... | collective-permute-start | bytes 221192 | tf_op jit(solution)/shard_map/ppermute | solution.py:246
  11.6 5.3 %collective-permute-start.4 = (bf16[72,512]{1,0:T(8,128)(2,1)S(1)}, bf16[72,512]{1,0:T(8,128)(2,1)S(1)}, u32[]{:S(2)}, u32[]{:S(2)}) collective-permute-start(bf16[72,512]{1,0:T(8,128)(2,1)S(1)} %collective-permute-done.2), channel_id=1, source_target_pairs={{0,4},{1,5},{2,6},{3,7},{4,0},{5,1},{6,2},{7,3},{8,12},{9,13},{10,... | collective-permute-start | bytes 221192 | tf_op jit(solution)/shard_map/ppermute | solution.py:246
  14.9 4.4 %collective-permute-start.5 = (bf16[72,512]{1,0:T(8,128)(2,1)S(1)}, bf16[72,512]{1,0:T(8,128)(2,1)S(1)}, u32[]{:S(2)}, u32[]{:S(2)}) collective-permute-start(bf16[72,512]{1,0:T(8,128)(2,1)S(1)} %collective-permute-done.3), channel_id=1, source_target_pairs={{0,4},{1,5},{2,6},{3,7},{4,0},{5,1},{6,2},{7,3},{8,12},{9,13},{10,... | collective-permute-start | bytes 221192 | tf_op jit(solution)/shard_map/ppermute | solution.py:246
  19.3 2.0 %collective-permute-start.6 = (bf16[576,512]{1,0:T(8,128)(2,1)S(1)}, bf16[576,512]{1,0:T(8,128)(2,1)S(1)}, u32[]{:S(2)}, u32[]{:S(2)}) collective-permute-start(bf16[576,512]{1,0:T(8,128)(2,1)S(1)} %constant_dynamic-update-slice_fusion.a_ref), channel_id=1, source_target_pairs={{0,1},{1,0},{2,3},{3,2},{4,5},{5,4},{6,7},{7,6},{8,9},{9,8},{10,11... | collective-permute-start | bytes 1769480 | tf_op jit(solution)/shard_map/ppermute | solution.py:246
  25.4 4.0 %collective-permute-start.7 = (bf16[72,256]{1,0:T(8,128)(2,1)S(1)}, bf16[72,256]{1,0:T(8,128)(2,1)S(1)}, u32[]{:S(2)}, u32[]{:S(2)}) collective-permute-start(bf16[72,256]{1,0:T(8,128)(2,1)S(1)} %get-tuple-element.23), channel_id=1, source_target_pairs={{0,2},{1,3},{2,0},{3,1},{4,6},{5,7},{6,4},{7,5},{8,10},{9,11},{10,... | collective-permute-start | bytes 110600 | tf_op jit(solution)/shard_map/ppermute | solution.py:246
